TPU v7x, 256 devices: a whole 4x4x8 slice. The times are simulated.
256 devices in a mesh: seq: 32 (over x, y, core), head: 8 (over z).
Axes of the slice: x: 4, y: 4, z: 8, core: 2. Of those that a mesh axis runs over, the one named last changes fastest.
Arguments:
- latent: bfloat16 [64, 4096], P('seq'), may hold values from -6 to 6
- pos_embed: bfloat16 [10752, 2048], P('seq', 'head'), may hold values from -3 to 3
- embed_weight: bfloat16 [32, 2048], P(None, 'head'), may hold values from -1 to 1
- norm_gain1: float32 [2048], replicated, may hold values from 0.1 to 1.9
- qkv_weight: bfloat16 [3, 2048, 2048], P(None, None, 'head'), may hold values from -1 to 1
- out_weight: bfloat16 [2048, 2048], P('head'), may hold values from -0.5 to 0.5
- norm_gain2: float32 [2048], replicated, may hold values from 0.1 to 1.9
- up_weight: bfloat16 [2048, 4096], P(None, 'head'), may hold values from -0.125 to 0.125
- down_weight: bfloat16 [4096, 2048], P('head'), may hold values from -0.09375 to 0.09375
Outputs:
- layer_out: bfloat16 [10752, 2048], P('seq', 'head')
All inputs are finite; a program needn't handle non-finite values.
Results may differ from a plain program's by a relative error of at most 0.02.
Values may be sent and summed in bfloat16 or wider, within the bound.
A program may use at most 128 MiB of HBM per device.

v0:
```python
import jax
import jax.numpy as jnp
from jax import lax
from jax.sharding import PartitionSpec as P

HS = 128
C = 32
W = 128


def rms_norm(values, gain):
    wide = values.astype(jnp.float32)
    scale = lax.rsqrt(jnp.mean(wide * wide, axis=-1, keepdims=True) + 1e-06)
    return (wide * scale * gain).astype(jnp.bfloat16)


def scale_level(positions, fine_count):
    return (positions >= fine_count // 16).astype(jnp.int32) + (
        positions >= fine_count // 16 + fine_count // 4
    ).astype(jnp.int32)


def pool_matrix(tok_start, count, pixel_rows, width, fine_count):
    positions = tok_start + jnp.arange(count, dtype=jnp.int32)
    first_end = fine_count // 16
    second_end = first_end + fine_count // 4
    offset_mid = positions - first_end
    offset_top = positions - second_end
    quarter = width // 4
    half = width // 2
    row_low = 4 * (positions // quarter)
    col_low = 4 * (positions % quarter)
    row_mid = 4 * (offset_mid // half // 2)
    col_mid = 4 * (offset_mid % half // 2)
    row_top = 2 * (offset_top // width // 2)
    col_top = 2 * (offset_top % width // 2)
    is_mid = positions >= first_end
    is_top = positions >= second_end
    row_first = jnp.where(is_top, row_top, jnp.where(is_mid, row_mid, row_low))
    col_first = jnp.where(is_top, col_top, jnp.where(is_mid, col_mid, col_low))
    block_side = jnp.where(is_top, 2, 4)
    share = jnp.where(is_top, 0.25, 0.0625).astype(jnp.float32)
    pixel_index = jnp.arange(pixel_rows * width, dtype=jnp.int32)
    pixel_row = pixel_index // width
    pixel_col = pixel_index % width
    inside_rows = (pixel_row[None, :] >= row_first[:, None]) & (
        pixel_row[None, :] < row_first[:, None] + block_side[:, None]
    )
    inside_cols = (pixel_col[None, :] >= col_first[:, None]) & (
        pixel_col[None, :] < col_first[:, None] + block_side[:, None]
    )
    return jnp.where(inside_rows & inside_cols, share[:, None], 0.0)


def body(
    latent,
    pos_embed,
    embed_weight,
    norm_gain1,
    qkv_weight,
    out_weight,
    norm_gain2,
    up_weight,
    down_weight,
):
    tok_rows = pos_embed.shape[0]
    local_width = pos_embed.shape[1]
    seq_count = lax.axis_size("seq")
    pixel_rows = latent.shape[0]
    fine_count = pixel_rows * seq_count * W
    seq_rank = lax.axis_index("seq")
    tok_first = seq_rank * tok_rows
    position_part = pos_embed.astype(jnp.float32)
    whole = lax.all_gather(latent, "seq", axis=0, tiled=True)
    pooling = pool_matrix(tok_first, tok_rows, whole.shape[0], W, fine_count).astype(jnp.bfloat16)
    inputs = jnp.dot(
        pooling, whole.reshape(whole.shape[0] * W, C), preferred_element_type=jnp.float32
    )
    stream = (
        jnp.dot(inputs, embed_weight.astype(jnp.float32), precision=lax.Precision.HIGHEST)
        + position_part
    ).astype(jnp.bfloat16)
    features = lax.all_gather(stream, "head", axis=1, tiled=True)
    normed = rms_norm(features, norm_gain1)
    projections = jnp.einsum(
        "td,jde->jte", normed, qkv_weight, preferred_element_type=jnp.float32
    ).astype(jnp.bfloat16)
    local_heads = local_width // HS
    queries = projections[0].reshape(tok_rows, local_heads, HS)
    query_levels = scale_level(tok_first + jnp.arange(tok_rows, dtype=jnp.int32), fine_count)
    inv_root = 1.0 / HS**0.5
    running = jnp.full((local_heads, tok_rows), -1e30, jnp.float32)
    key_piece = lax.all_gather(projections[1], "seq", axis=0, tiled=True)
    value_piece = lax.all_gather(projections[2], "seq", axis=0, tiled=True)
    count = key_piece.shape[0]
    key_heads = key_piece.reshape(count, local_heads, HS)
    value_heads = value_piece.reshape(count, local_heads, HS)
    scores = (
        jnp.einsum("qhe,khe->hqk", queries, key_heads, preferred_element_type=jnp.float32)
        * inv_root
    )
    key_levels = scale_level(jnp.arange(count, dtype=jnp.int32), fine_count)
    allowed = (key_levels[None, :] <= query_levels[:, None])[None]
    scores = jnp.where(allowed, scores, -1e30)
    newest = jnp.maximum(running, jnp.max(scores, axis=-1))
    raw = jnp.where(allowed, jnp.exp(scores - newest[..., None]), 0.0)
    totals = jnp.sum(raw, axis=-1)
    contrib = jnp.einsum(
        "hqk,khe->hqe", raw.astype(jnp.bfloat16), value_heads, preferred_element_type=jnp.float32
    )
    accum = contrib
    running, totals, accum = (newest, totals, accum)
    attended = (
        (accum / totals[..., None])
        .transpose(1, 0, 2)
        .reshape(tok_rows, local_width)
        .astype(jnp.bfloat16)
    )
    partial_out = jnp.dot(attended, out_weight, preferred_element_type=jnp.float32)
    head_rank = lax.axis_index("head")
    summed_out = lax.psum(partial_out.astype(jnp.bfloat16), "head").astype(jnp.float32)
    mixed = (features.astype(jnp.float32) + summed_out).astype(jnp.bfloat16)
    own_mixed = lax.dynamic_slice_in_dim(mixed, head_rank * local_width, local_width, 1)
    normed2 = rms_norm(mixed, norm_gain2)
    hidden = jax.nn.gelu(
        jnp.dot(normed2, up_weight, preferred_element_type=jnp.float32), approximate=True
    ).astype(jnp.bfloat16)
    partial_mlp = jnp.dot(hidden, down_weight, preferred_element_type=jnp.float32)
    mlp_share = lax.psum_scatter(
        partial_mlp.astype(jnp.bfloat16), "head", scatter_dimension=1, tiled=True
    ).astype(jnp.float32)
    return (own_mixed.astype(jnp.float32) + mlp_share).astype(jnp.bfloat16)


def solution(mesh):
    in_specs = (
        P("seq", None),
        P("seq", "head"),
        P(None, "head"),
        P(),
        P(None, None, "head"),
        P("head", None),
        P(),
        P(None, "head"),
        P("head", None),
    )
    out_specs = P("seq", "head")
    return jax.shard_map(body, mesh=mesh, in_specs=in_specs, out_specs=out_specs, check_vma=False)
```

profile of v0, /device:TPU:6, one launch (start us, length us, event | category | flops | bytes accessed | tf_op | source)
XLA Modules:
  0.0 362.4 jit_solution(8283692721358141733)
XLA Ops:
  6.5 0.0 copy-start
  6.5 0.0 all-gather.7.cloned.1.call-start
  6.6 27.3 %all-gather.2 = bf16[32,2,4096]{2,1,0:T(2,128)(2,1)} all-gather(bf16[1,2,4096]{2,1,0:T(2,128)(2,1)} %bitcast.31), channel_id=1, replica_groups=mesh['seq'=32,'head'=8] {'seq'}, dimensions={0}, use_global_device_ids=true | all-gather | bytes 540672 | tf_op jit(solution)/shard_map/all_gather | solution.py:74
  33.9 3.8 %reshape.266 = bf16[8192,32]{1,0:T(8,128)(2,1)} reshape(bf16[32,2,4096]{2,1,0:T(2,128)(2,1)} %all-gather.2) | data formatting | bytes 1048576 | tf_op jit(solution)/shard_map/reshape | solution.py:77
  37.7 0.0 copy-start.4
  37.7 0.0 copy-start.5
  37.7 0.0 copy-start.6
  37.7 4.8 %fusion.9 = f32[336,32]{0,1:T(8,128)S(1)} fusion(bf16[8192,32]{1,0:T(8,128)(2,1)} %reshape.266, bf16[336]{0:T(512)(128)(2,1)S(1)} %broadcast_select_fusion, s32[8192]{0:T(1024)S(1)} %get-tuple-element.16, s32[8192]{0:T(1024)S(1)} %get-tuple-element.17, s32[336]{0:T(512)S(1)} %get-tuple-element.12, s32[336]{0:T(512)S(1)} %get-tuple-element.15, ...), kind=kOutput, calls=%fused_computation.12 | convolution fusion | flops 198180864 | bytes 638880 | tf_op jit(solution)/shard_map/dot_general | solution.py:76
  42.5 0.0 copy-done.4
  42.5 0.0 copy-done.5
  42.6 1.0 fusion.41
  43.6 0.0 all-gather.7.cloned.1.call-update
  43.6 0.0 all-gather.9.cloned.1.call-start
  43.7 43.4 %all-gather.7.cloned.1.call-done = bf16[336,2048]{1,0:T(8,128)(2,1)} async-done(((bf16[336,256]{1,0:T(8,128)(2,1)}), bf16[336,2048]{1,0:T(8,128)(2,1)}) %all-gather.7.cloned.1.call-update) | async-done | bytes 1376272 | tf_op jit(solution)/shard_map/all_gather | solution.py:83
  87.0 1.7 fusion.17
  88.7 0.0 copy-done
  88.8 0.0 copy-done.6
  88.8 2.6 fusion.33
  91.4 0.8 fusion.125
  92.2 0.0 all-gather.9.cloned.1.call-update
  92.2 0.0 all-gather.11.cloned.1.call-start
  92.2 0.7 all-gather.11.cloned.1.call-update
  92.9 0.2 all-reduce.2.cloned.1.call-start
  93.2 3.7 %broadcast_compare_fusion = pred[336,10752]{1,0:T(8,128)(4,1)} fusion(s32[10752]{0:T(1024)S(1)} %convert_add_fusion.1, s32[336]{0:T(512)S(1)} %convert_add_fusion.2), kind=kLoop, calls=%fused_computation.8 | loop fusion | flops 3612672 | bytes 3657024 | tf_op jit(solution)/shard_map/le | solution.py:103
  96.9 46.6 %all-gather.9.cloned.1.call-done = bf16[1,10752,256]{2,1,0:T(8,128)(2,1)} async-done(((bf16[1,336,256]{2,1,0:T(8,128)(2,1)}), bf16[1,10752,256]{2,1,0:T(8,128)(2,1)}) %all-gather.9.cloned.1.call-update) | async-done | bytes 5505040 | tf_op jit(solution)/shard_map/all_gather | solution.py:93
  143.6 11.4 %reshape.267 = bf16[10752,2,128]{2,1,0:T(2,128)(2,1)} reshape(bf16[1,10752,256]{2,1,0:T(8,128)(2,1)} %all-gather.9.cloned.1.call-done) | data formatting | bytes 11010048 | tf_op jit(solution)/shard_map/reshape | solution.py:96
  154.9 15.9 %fusion = (f32[2,336]{1,0:T(2,128)S(1)}, f32[2,336,10752]{2,1,0:T(8,128)}) fusion(pred[336,10752]{1,0:T(8,128)(4,1)} %broadcast_compare_fusion, bf16[10752,2,128]{2,1,0:T(2,128)(2,1)} %reshape.267, bf16[336,2,128]{2,1,0:T(2,128)(2,1)S(1)} %reshape_squeeze.3), kind=kOutput, calls=%fused_computation.2 | convolution fusion | flops 1871363456 | bytes 38193792 | tf_op jit(solution)/shard_map/qhe,khe->hqk/dot_general | solution.py:99
  170.9 14.8 %fusion.1 = f32[2,336]{1,0:T(2,128)S(1)} fusion(f32[2,336,10752]{2,1,0:T(8,128)} %get-tuple-element.11, f32[2,336]{1,0:T(2,128)S(1)} %broadcast_maximum_fusion, pred[336,10752]{1,0:T(8,128)(4,1)} %broadcast_compare_fusion), kind=kLoop, calls=%fused_computation.3 | loop fusion | flops 36126048 | bytes 32519424 | tf_op jit(solution)/shard_map/reduce_sum | solution.py:107
  185.6 12.7 %all-gather.11.cloned.1.call-done = bf16[1,10752,256]{2,1,0:T(8,128)(2,1)} async-done(((bf16[1,336,256]{2,1,0:T(8,128)(2,1)}), bf16[1,10752,256]{2,1,0:T(8,128)(2,1)}) %all-gather.11.cloned.1.call-update) | async-done | bytes 5505040 | tf_op jit(solution)/shard_map/all_gather | solution.py:94
  198.3 11.4 %reshape.268 = bf16[10752,2,128]{2,1,0:T(2,128)(2,1)} reshape(bf16[1,10752,256]{2,1,0:T(8,128)(2,1)} %all-gather.11.cloned.1.call-done) | data formatting | bytes 11010048 | tf_op jit(solution)/shard_map/reshape | solution.py:97
  209.7 0.0 copy-start.3
  209.7 17.9 %fusion.52 = bf16[2,42,8,128]{3,2,1,0:T(8,128)(2,1)S(1)} fusion(bf16[10752,2,128]{2,1,0:T(2,128)(2,1)} %reshape.268, f32[2,336,10752]{2,1,0:T(8,128)} %get-tuple-element.11, f32[2,336]{1,0:T(2,128)S(1)} %broadcast_maximum_fusion, pred[336,10752]{1,0:T(8,128)(4,1)} %broadcast_compare_fusion, f32[336,2]{0,1:T(2,128)S(1)} %bitcast.32), kind=kOutput, calls=%fused_computation.46 | convolution fusion | flops 1885986816 | bytes 38196480 | tf_op jit(solution)/shard_map/hqk,khe->hqe/dot_general | solution.py:108
  227.6 0.0 copy-done.3
  227.6 0.0 copy-start.2
  227.6 1.6 convolution_convert_fusion.1
  229.2 0.0 copy-start.7
  229.2 0.0 all-reduce.2.cloned.1.call-update
  229.2 0.0 reduce-scatter.2.cloned.1.call-start
  229.3 77.4 %all-reduce.2.cloned.1.call-done = bf16[336,2048]{1,0:T(8,128)(2,1)} async-done(((bf16[336,2048]{1,0:T(8,128)(2,1)}), bf16[336,2048]{1,0:T(8,128)(2,1)}) %all-reduce.2.cloned.1.call-update) | async-done | bytes 1376272 | tf_op jit(solution)/shard_map/psum | solution.py:121
  306.7 0.0 copy-done.2
  306.7 2.9 fusion.14
  309.6 0.0 copy-done.7
  309.6 0.0 copy-start.1
  309.6 5.7 %convolution_convert_fusion = bf16[336,2048]{1,0:T(8,128)(2,1)} fusion(bf16[512,2048]{1,0:T(8,128)(2,1)} %param.17, bf16[2048,512]{1,0:T(8,128)(2,1)} %param.16, bf16[336,2048]{1,0:T(8,128)(2,1)} %get-tuple-element.6, f32[2048]{0:T(1024)S(1)} %copy-done.7, f32[336]{0:T(512)S(1)} %add_rsqrt_fusion), kind=kOutput, calls=%fused_computation.29 | convolution fusion | flops 1414275072 | bytes 6956352 | tf_op jit(solution)/shard_map/dot_general | solution.py:128
  315.3 0.0 reduce-scatter.2.cloned.1.call-update
  315.4 38.8 %reduce-scatter.2.cloned.1.call-done = bf16[336,256]{1,0:T(8,128)(2,1)} async-done(((bf16[336,2048]{1,0:T(8,128)(2,1)}), bf16[336,256]{1,0:T(8,128)(2,1)}) %reduce-scatter.2.cloned.1.call-update) | async-done | bytes 172048 | tf_op jit(solution)/shard_map/reduce_scatter | solution.py:129
  354.2 1.7 add_convert_fusion
  355.9 0.0 copy-done.1
  (10 shorter events, 0.2 us)
Async XLA Ops:
  6.5 82.2 %copy-start = (bf16[3,2048,256]{2,1,0:T(8,128)(2,1)S(1)}, bf16[3,2048,256]{2,1,0:T(8,128)(2,1)}, u32[]{:S(2)}) copy-start(bf16[3,2048,256]{2,1,0:T(8,128)(2,1)} %param.13) | copy-start | bytes 9437188
  6.5 80.5 %all-gather.7.cloned.1.call-start = ((), (), s32[]{:S(2)}) async-start(), calls=%async_computation.1 | async-start | bytes 1548288 | tf_op jit(solution)/shard_map/all_gather | solution.py:83
  37.7 4.8 %copy-start.4 = (bf16[336,256]{1,0:T(8,128)(2,1)S(1)}, bf16[336,256]{1,0:T(8,128)(2,1)}, u32[]{:S(2)}) copy-start(bf16[336,256]{1,0:T(8,128)(2,1)} %param.10) | copy-start | bytes 516100
  37.7 4.8 %copy-start.5 = (bf16[32,256]{1,0:T(8,128)(2,1)S(1)}, bf16[32,256]{1,0:T(8,128)(2,1)}, u32[]{:S(2)}) copy-start(bf16[32,256]{1,0:T(8,128)(2,1)} %param.11) | copy-start | bytes 49156
  37.7 51.0 %copy-start.6 = (f32[2048]{0:T(1024)S(1)}, f32[2048]{0:T(1024)}, u32[]{:S(2)}) copy-start(f32[2048]{0:T(1024)} %param.12) | copy-start | bytes 24580
  43.6 99.9 %all-gather.9.cloned.1.call-start = ((), (), s32[]{:S(2)}) async-start(), calls=%async_computation.4 | async-start | bytes 5677056 | tf_op jit(solution)/shard_map/all_gather | solution.py:93
  92.2 106.1 %all-gather.11.cloned.1.call-start = ((), (), s32[]{:S(2)}) async-start(), calls=%async_computation.5 | async-start | bytes 5677056 | tf_op jit(solution)/shard_map/all_gather | solution.py:94
  92.9 213.8 %all-reduce.2.cloned.1.call-start = ((), (), s32[]{:S(2)}) async-start(), calls=%async_computation.2 | async-start | bytes 2752512 | tf_op jit(solution)/shard_map/psum | solution.py:121
  209.7 17.9 %copy-start.3 = (bf16[256,2048]{1,0:T(8,128)(2,1)S(1)}, bf16[256,2048]{1,0:T(8,128)(2,1)}, u32[]{:S(2)}) copy-start(bf16[256,2048]{1,0:T(8,128)(2,1)} %param.14) | copy-start | bytes 3145732
  227.6 79.1 %copy-start.2 = (bf16[336,2048]{1,0:T(8,128)(2,1)S(1)}, bf16[336,2048]{1,0:T(8,128)(2,1)}, u32[]{:S(2)}) copy-start(bf16[336,2048]{1,0:T(8,128)(2,1)} %all-gather.7.cloned.1.call-done) | copy-start | bytes 4128772
  229.2 80.4 %copy-start.7 = (f32[2048]{0:T(1024)S(1)}, f32[2048]{0:T(1024)}, u32[]{:S(2)}) copy-start(f32[2048]{0:T(1024)} %param.15) | copy-start | bytes 24580
  229.2 124.9 %reduce-scatter.2.cloned.1.call-start = ((), (), s32[]{:S(2)}) async-start(), calls=%async_computation.3 | async-start | bytes 1548288 | tf_op jit(solution)/shard_map/reduce_scatter | solution.py:129
  309.6 46.2 %copy-start.1 = (bf16[3,2048,256]{2,1,0:T(8,128)(2,1)S(1)}, bf16[3,2048,256]{2,1,0:T(8,128)(2,1)}, u32[]{:S(2)}) copy-start(bf16[3,2048,256]{2,1,0:T(8,128)(2,1)} %param.13) | copy-start | bytes 9437188
Sparse Core Ops, SparseCore 0:
  43.7 43.2 all-gather.6
  92.3 51.2 all-gather.8
  146.1 52.1 all-gather.10
  229.4 77.3 all-reduce.1
  315.5 38.6 reduce-scatter.1
where the time goes:
time: 363 us; the launch traced here: 362 us
  waiting for transfers between devices  220 us (61%)
  matrix products  49.6 us (14%)
  local copies, waits for them, and re-layouts  27.4 us (8%)
  blocking collectives  27.3 us (8%)
  other arithmetic  24.9 us (7%)
  between operations  13.3 us (4%)
    psum x1, waiting for transfers between devices, body(): lax.psum(partial_out.astype(jnp.bfloat16), 'head').astype(jnp.float32)  77.4 us
    all_gather x1, waiting for transfers between devices, body(): key_piece = lax.all_gather(projections[1], 'seq', axis=0, tiled=True)  46.6 us
    all_gather x1, waiting for transfers between devices, body(): features = lax.all_gather(stream, 'head', axis=1, tiled=True)  43.4 us
    reduce_scatter x1, waiting for transfers between devices, body(): lax.psum_scatter(partial_mlp.astype(jnp.bfloat16), 'head', scatter_dimens...  38.8 us
    all_gather x1, blocking collectives, body(): whole = lax.all_gather(latent, 'seq', axis=0, tiled=True)  27.3 us
    dot_general x1, matrix products, body(): jnp.einsum('hqk,khe->hqe', raw.astype(jnp.bfloat16), value_heads, preferr...  17.9 us
    dot_general x1, matrix products, body(): jnp.einsum('qhe,khe->hqk', queries, key_heads, preferred_element_type=jnp...  15.9 us
    reduce_sum x1, other arithmetic, body(): totals = jnp.sum(raw, axis=-1)  14.8 us
  transfers between devices with their start and end apart: 5, of which 5 were waited for; matrix products, arithmetic and copies ran while one was open for 13% of the time, Pallas kernels for 0%

commit v1 on v0

v1 whole, which is shorter than its diff:
```python
import functools

import jax
import jax.numpy as jnp
from jax import lax
from jax.experimental import pallas as pl
from jax.experimental.pallas import tpu as pltpu
from jax.sharding import PartitionSpec as P

D = 2048
HS = 128
C = 32
TOK = 336
FB = 256
HID = 512
FIRST = 512
SECOND = 2560
PARTS = 1
R = TOK // PARTS
MSG = R + 16
NCH = (R + 127) // 128
NZ = 8
KEYS = 8 * TOK
NEG = -1e30
QSCALE = 1.4426950408889634 / HS**0.5
MESH = pl.DeviceIdType.MESH
BF = jnp.bfloat16
F32 = jnp.float32
NT = (((1,), (1,)), ((), ()))


def split3(wide):
    high = wide.astype(BF)
    rest = wide - high.astype(F32)
    mid = rest.astype(BF)
    low = (rest - mid.astype(F32)).astype(BF)
    return high, mid, low


def level(token):
    return (token >= FIRST).astype(jnp.int32) + (token >= SECOND).astype(jnp.int32)


def halves(rows):
    first = (rows // 32) * 16
    return pl.ds(0, first), pl.ds(first, rows - first)


def kernel(
    cells_ref,
    pos_hbm,
    embed_hbm,
    gain1_ref,
    qkv_hbm,
    out_w_hbm,
    gain2_ref,
    up_hbm,
    down_hbm,
    out_ref,
    wqkv,
    wout,
    wup,
    wdown,
    grid_cells,
    pos_all,
    emb_all,
    inp,
    own_stream,
    acc,
    ssq,
    kv_send,
    q_send,
    kv_buf,
    q_buf,
    o_send,
    o_recv,
    state_o,
    state_m,
    attended,
    rs_send,
    rs_recv,
    mixed_all,
    acc2,
    ssq2,
    hidden,
    local_sem,
    cell_sem,
    pos_sem,
    emb_sem,
    kv_ssem,
    kv_rsem,
    q_ssem,
    q_rsem,
    o_ssem,
    o_rsem,
    rs_sem,
    mix_sem,
):
    seq = lax.axis_index("seq")
    z = lax.axis_index("head")
    x, y, c = seq // 8, lax.rem(seq // 2, 4), lax.rem(seq, 2)
    right, left = lax.rem(z + 1, NZ), lax.rem(z + NZ - 1, NZ)
    a0 = jnp.where(c == 0, x, y)
    b0 = jnp.where(c == 0, y, x)

    def sid(px, py, pc):
        return (px * 4 + py) * 2 + pc

    def ring(value, step):
        return lax.rem(value + step, 4)

    sibling = sid(x, y, 1 - c)

    loads = [
        pltpu.make_async_copy(pos_hbm.at[pl.ds(p * R, R)], pos_all.at[p, z], local_sem.at[p])
        for p in range(PARTS)
    ]
    loads.append(pltpu.make_async_copy(embed_hbm, emb_all.at[z], local_sem.at[PARTS]))
    weights = [
        pltpu.make_async_copy(src, dst, local_sem.at[PARTS + 1 + i])
        for i, (src, dst) in enumerate(
            ((qkv_hbm, wqkv), (out_w_hbm, wout), (up_hbm, wup), (down_hbm, wdown))
        )
    ]
    for load in loads:
        load.start()
    for load in weights:
        load.start()

    barrier = pltpu.get_barrier_semaphore()
    pl.semaphore_signal(barrier, inc=1, device_id={"head": right}, device_id_type=MESH)
    pl.semaphore_signal(barrier, inc=1, device_id={"head": left}, device_id_type=MESH)
    pl.semaphore_signal(barrier, inc=1, device_id={"seq": sibling}, device_id_type=MESH)
    for step in (1, 2, 3):
        for core in (0, 1):
            for peer in (sid(ring(x, step), y, core), sid(x, ring(y, step), core)):
                pl.semaphore_signal(barrier, inc=1, device_id={"seq": peer}, device_id_type=MESH)
    pl.semaphore_wait(barrier, 15)

    def remote(src, dst, ssem, rsem, **where):
        return pltpu.make_async_remote_copy(
            src_ref=src,
            dst_ref=dst,
            send_sem=ssem,
            recv_sem=rsem,
            device_id=where,
            device_id_type=MESH,
        )

    def ag_copies(buf, sems, rows, k):
        go, back = lax.rem(z + NZ - k, NZ), lax.rem(z + k, NZ)
        if k == 3:
            upper, lower = halves(rows)
        else:
            upper = lower = pl.ds(0, rows)
        return (
            remote(buf.at[go, upper], buf.at[go, upper], sems.at[0, k, 0], sems.at[0, k, 1], head=right),
            remote(buf.at[back, lower], buf.at[back, lower], sems.at[1, k, 0], sems.at[1, k, 1], head=left),
        )

    def ag_start(buf, sems, rows, k):
        for copy in ag_copies(buf, sems, rows, k):
            copy.start()

    def ag_wait(buf, sems, rows, k):
        for copy in ag_copies(buf, sems, rows, k):
            copy.wait_recv()

    def ag_drain(buf, sems, rows):
        for k in range(4):
            for copy in ag_copies(buf, sems, rows, k):
                copy.wait_send()

    pos_args = [(pos_all.at[p], pos_sem.at[p], R) for p in range(PARTS)]
    emb_args = (emb_all, emb_sem, C)
    mix_args = [(mixed_all.at[p], mix_sem.at[p], R) for p in range(PARTS)]

    for load in loads:
        load.wait()
    ag_start(*emb_args, 0)
    for p in range(PARTS):
        ag_start(*pos_args[p], 0)

    grid_cells[c, x, y] = cells_ref[...]
    along_y = [
        remote(
            grid_cells.at[c, x, y],
            grid_cells.at[c, x, y],
            cell_sem.at[step - 1, 0],
            cell_sem.at[step - 1, 1],
            seq=sid(x, ring(y, step), c),
        )
        for step in (1, 2, 3)
    ]
    for copy in along_y:
        copy.start()
    for copy in along_y:
        copy.wait_recv()
    along_x = [
        remote(
            grid_cells.at[c, x],
            grid_cells.at[c, x],
            cell_sem.at[2 + step, 0],
            cell_sem.at[2 + step, 1],
            seq=sid(ring(x, step), y, c),
        )
        for step in (1, 2, 3)
    ]
    for copy in along_x:
        copy.start()
    for copy in along_x:
        copy.wait_recv()
    across = remote(
        grid_cells.at[c], grid_cells.at[c], cell_sem.at[6, 0], cell_sem.at[6, 1], seq=sibling
    )
    across.start()

    token = seq * TOK + lax.broadcasted_iota(jnp.int32, (TOK, 1), 0)
    top, mid_level = token >= SECOND, token >= FIRST
    from_top, from_mid = token - SECOND, token - FIRST
    key_top = (from_top >> 8) * 64 + ((from_top & 127) >> 1)
    key_mid = (from_mid >> 7) * 32 + ((from_mid & 63) >> 1)
    fine_key = jnp.where(top, key_top, -1)
    coarse_key = jnp.where(top, -1, jnp.where(mid_level, key_mid, token))
    col = lax.broadcasted_iota(jnp.int32, (1, 2048), 1)
    cell_row = ((col >> 8) & 3) * 8 + ((col >> 6) & 3) * 2 + (col >> 10)
    cell_col = col & 63
    fine_col = cell_row * 64 + cell_col
    coarse_col = (cell_row >> 1) * 32 + (cell_col >> 1)
    select = jnp.where(
        fine_key == fine_col, 1.0, jnp.where(coarse_key == coarse_col, 0.25, 0.0)
    ).astype(BF)
    across.wait_recv()
    pooled = jnp.dot(
        select, grid_cells[...].reshape(2048, 128), preferred_element_type=F32
    )
    inputs = pooled[:, 0:C] + pooled[:, C : 2 * C] + pooled[:, 2 * C : 3 * C]
    for i, piece in enumerate(split3(inputs)):
        inp[i] = piece

    def embed_block(p, f, own=False):
        rows = pl.ds(p * R, R)
        emb = emb_all[f]
        wide = pos_all[p, f].astype(F32)
        for i in range(3):
            wide = wide + jnp.dot(inp[i, rows, :], emb, preferred_element_type=F32)
        stream = wide.astype(BF)
        if own:
            own_stream[rows, :] = stream
        wide = stream.astype(F32)
        square = wide * wide
        square = square[:, :128] + square[:, 128:]
        lanes = pl.ds(pl.multiple_of(f * FB, FB), FB)
        normed = (wide * gain1_ref[:, lanes]).astype(BF)
        for j in range(3):
            piece = jnp.dot(normed, wqkv[j, lanes, :], preferred_element_type=F32)
            if own:
                acc[rows, j * FB : (j + 1) * FB] = piece
            else:
                acc[rows, j * FB : (j + 1) * FB] += piece
        if own:
            ssq[rows, :] = square
        else:
            ssq[rows, :] += square

    def project(p):
        rows = pl.ds(p * R, R)
        total = jnp.sum(ssq[rows, :], axis=1, keepdims=True)
        scale = lax.rsqrt(total * (1.0 / D) + 1e-6)
        for h in range(2):
            cols = slice(h * HS, (h + 1) * HS)
            q_send[h, rows, :] = (acc[rows, cols] * (scale * QSCALE)).astype(BF)
            kv_send[h, rows, 0:HS] = (acc[rows, FB + h * HS : FB + (h + 1) * HS] * scale).astype(BF)
            kv_send[h, rows, HS:] = (
                acc[rows, 2 * FB + h * HS : 2 * FB + (h + 1) * HS] * scale
            ).astype(BF)

    def slot_rows(slot, p):
        return pl.ds(pl.multiple_of(slot * TOK + p * R, 16), R)

    def exchange(p):
        rows = pl.ds(p * R, R)
        kv_copies, q_copies = [], []

        def kv_copy(i, head, slot, dest):
            return remote(
                kv_send.at[head, rows],
                kv_buf.at[slot_rows(slot, p)],
                kv_ssem.at[p, i],
                kv_rsem.at[p, slot],
                seq=dest,
            )

        def q_copy(i, head, slot, dest):
            return remote(
                q_send.at[head, rows],
                q_buf.at[p, slot],
                q_ssem.at[p, i],
                q_rsem.at[p, slot],
                seq=dest,
            )

        other = 1 - c
        kv_copies.append(kv_copy(6, other, jnp.where(c == 1, x, y) * 2 + c, sibling))
        q_copies.append(q_copy(6, other, jnp.where(c == 1, y, x) * 2 + c, sibling))
        for i, step in enumerate((1, 3, 2)):
            kv_copies.append(kv_copy(i, 0, x * 2 + c, sid(ring(x, step), y, 0)))
            kv_copies.append(kv_copy(3 + i, 1, y * 2 + c, sid(x, ring(y, step), 1)))
            q_copies.append(q_copy(i, 0, y * 2 + c, sid(x, ring(y, step), 0)))
            q_copies.append(q_copy(3 + i, 1, x * 2 + c, sid(ring(x, step), y, 1)))
        return kv_copies, q_copies

    def exchange_start(p):
        rows = pl.ds(p * R, R)
        kv_copies, q_copies = exchange(p)
        for copy in q_copies + kv_copies:
            copy.start()
        kv_buf[slot_rows(a0 * 2 + c, p), :] = kv_send[c, rows, :]
        q_buf[p, b0 * 2 + c] = q_send[c, rows, :]

    def exchange_wait(p, want_q, want_kv):
        rows = pl.ds(p * R, R)
        for i in range(1, 8):
            if want_q:
                slot = lax.rem(b0 * 2 + c + i, 8)
                remote(
                    q_send.at[0, rows],
                    q_buf.at[p, slot],
                    q_ssem.at[p, 0],
                    q_rsem.at[p, slot],
                    seq=sibling,
                ).wait_recv()
            if want_kv:
                slot = lax.rem(a0 * 2 + c + i, 8)
                remote(
                    kv_send.at[0, rows],
                    kv_buf.at[slot_rows(slot, p)],
                    kv_ssem.at[p, 0],
                    kv_rsem.at[p, slot],
                    seq=sibling,
                ).wait_recv()

    def exchange_drain(p):
        kv_copies, q_copies = exchange(p)
        for copy in q_copies + kv_copies:
            copy.wait_send()

    ones_row = jnp.ones((1, HS), BF)

    def values_and_ones(kv):
        return jnp.concatenate([kv[:, HS:], jnp.broadcast_to(ones_row, (kv.shape[0], HS))], axis=1)

    diag = lax.broadcasted_iota(jnp.int32, (128, 128), 0) == lax.broadcasted_iota(
        jnp.int32, (128, 128), 1
    )

    def finish(p, first, count, total, largest):
        sums = total[:, HS:]
        sums = jnp.where(sums > 0.0, sums, 1.0)
        normal = (total[:, :HS] / sums).astype(BF)
        log_sum = largest + jnp.log2(sums)
        for i in range(count):
            o_send[p, first + i, 0:R, :] = normal[i * R : (i + 1) * R]
            lines = []
            for j in range(NCH):
                low, high = i * R + j * 128, i * R + min((j + 1) * 128, R)
                tile = log_sum[low:high]
                if high - low < 128:
                    tile = jnp.concatenate(
                        [tile, jnp.zeros((128 - (high - low), 128), F32)], axis=0
                    )
                lines.append(jnp.sum(jnp.where(diag, tile, 0.0), axis=0, keepdims=True))
            line = jnp.concatenate(lines, axis=0) if NCH > 1 else lines[0]
            high_part, mid_part, low_part = split3(line)
            packed = [v.astype(F32) for v in (high_part, mid_part, low_part)]
            packed.append(jnp.zeros((16 - 3 * NCH, 128), F32))
            o_send[p, first + i, R:MSG, :] = jnp.concatenate(packed, axis=0).astype(BF)

    KC = 896

    def full_tile(p, first, count):
        queries = q_buf[p, pl.ds(first, count)].reshape(count * R, HS)
        largest = total = None
        for j in range(KEYS // KC):
            kv = kv_buf[j * KC : (j + 1) * KC, :]
            scores = lax.dot_general(queries, kv[:, :HS], NT, preferred_element_type=F32)
            newest = jnp.max(scores, axis=1, keepdims=True)
            if total is not None:
                newest = jnp.maximum(newest, largest)
            weights = jnp.exp2(scores - newest).astype(BF)
            part = jnp.dot(weights, values_and_ones(kv), preferred_element_type=F32)
            total = part if total is None else total * jnp.exp2(largest - newest) + part
            largest = newest
        finish(p, first, count, total, largest)

    def masked_tile(p, b, first_q):
        rows = 2 * R
        first = b * 2
        state_m[...] = jnp.full((rows, 128), NEG, F32)
        state_o[...] = jnp.zeros((rows, 2 * HS), F32)
        line = lax.broadcasted_iota(jnp.int32, (rows, 1), 0)
        second = (line >= R).astype(jnp.int32)
        q_level = level((first_q + second) * TOK + p * R + line - second * R)
        top_level = level((first_q + 1) * TOK + TOK - 1)

        @pl.loop(0, 4)
        def _(a):
            first_k = jnp.where(c == 0, a * 8 + y * 2, x * 8 + a * 2)

            @pl.when(level(first_k * TOK) <= top_level)
            def _():
                kv = kv_buf[pl.ds(pl.multiple_of(a * 2 * TOK, 16), 2 * TOK), :]
                queries = q_buf[p, pl.ds(first, 2)].reshape(rows, HS)
                scores = lax.dot_general(queries, kv[:, :HS], NT, preferred_element_type=F32)
                k_level = level(
                    first_k * TOK + lax.broadcasted_iota(jnp.int32, (1, 2 * TOK), 1)
                )
                scores = jnp.where(k_level <= q_level, scores, NEG)
                before = state_m[:, 0:1]
                newest = jnp.maximum(before, jnp.max(scores, axis=1, keepdims=True))
                weights = jnp.exp2(scores - newest).astype(BF)
                part = jnp.dot(weights, values_and_ones(kv), preferred_element_type=F32)
                state_o[...] = state_o[...] * jnp.exp2(before - newest) + part
                state_m[...] = jnp.broadcast_to(newest, (rows, 128))

        finish(p, first, 2, state_o[...], state_m[:, 0:1])

    def attend(p):
        everything = jnp.logical_and(c == 0, x >= 1)

        @pl.when(everything)
        def _():
            @pl.loop(0, 2)
            def _(i):
                full_tile(p, i * 4, 2)
                full_tile(p, i * 4 + 2, 2)

        @pl.when(jnp.logical_not(everything))
        def _():
            @pl.loop(0, 4)
            def _(b):
                first_q = jnp.where(c == 0, x * 8 + b * 2, b * 8 + y * 2)
                plain = first_q >= 8

                @pl.when(plain)
                def _():
                    full_tile(p, b * 2, 2)

                @pl.when(jnp.logical_not(plain))
                def _():
                    masked_tile(p, b, first_q)

    def give_copies(p):
        copies = [
            remote(
                o_send.at[p, b0 * 2 + 1 - c],
                o_recv.at[p, c * 4 + b0],
                o_ssem.at[p, 6],
                o_rsem.at[p, c * 4 + b0],
                seq=sibling,
            )
        ]
        for i, step in enumerate((1, 3, 2)):
            b = ring(b0, step)
            for core in (0, 1):
                dest = jnp.where(c == 0, sid(x, b, core), sid(b, y, core))
                copies.append(
                    remote(
                        o_send.at[p, b * 2 + core],
                        o_recv.at[p, c * 4 + b0],
                        o_ssem.at[p, i * 2 + core],
                        o_rsem.at[p, c * 4 + b0],
                        seq=dest,
                    )
                )
        return copies

    def give_start(p):
        for copy in give_copies(p):
            copy.start()
        o_recv[p, c * 4 + b0] = o_send[p, b0 * 2 + c]

    def give_wait(p):
        for i in range(1, 8):
            slot = lax.rem(c * 4 + b0 + i, 8)
            remote(
                o_send.at[p, 0],
                o_recv.at[p, slot],
                o_ssem.at[p, 0],
                o_rsem.at[p, slot],
                seq=sibling,
            ).wait_recv()

    def give_drain(p):
        for copy in give_copies(p):
            copy.wait_send()

    def combine(p):
        tails = [o_recv[p, i, R:MSG, :].astype(F32) for i in range(8)]
        for j in range(NCH):
            low, high = j * 128, min((j + 1) * 128, R)
            logs = [
                t[j : j + 1] + t[NCH + j : NCH + j + 1] + t[2 * NCH + j : 2 * NCH + j + 1]
                for t in tails
            ]
            shares = []
            for h in range(2):
                four = logs[h * 4 : h * 4 + 4]
                largest = functools.reduce(jnp.maximum, four)
                powers = [jnp.exp2(v - largest) for v in four]
                total = powers[0] + powers[1] + powers[2] + powers[3]
                shares += [v / total for v in powers]
            for h in range(2):
                mean = None
                for a in range(4):
                    share = jnp.sum(
                        jnp.where(diag, shares[h * 4 + a], 0.0), axis=1, keepdims=True
                    )
                    term = o_recv[p, h * 4 + a, low:high, :].astype(F32) * share[: high - low]
                    mean = term if mean is None else mean + term
                attended[p * R + low : p * R + high, h * HS : (h + 1) * HS] = mean.astype(BF)

    def rs_copies(p, phase, k):
        upper, lower = halves(R)
        if k > 0:
            upper = lower = pl.ds(0, R)
        send, recv, sems = rs_send.at[phase, p], rs_recv.at[phase, p], rs_sem.at[phase, p]
        return (
            remote(send.at[0, k, upper], recv.at[0, k, upper], sems.at[0, k, 0], sems.at[0, k, 1], head=right),
            remote(send.at[1, k, lower], recv.at[1, k, lower], sems.at[1, k, 0], sems.at[1, k, 1], head=left),
        )

    def rs_step(p, phase, block, k):
        upper, lower = halves(R)
        send, recv = rs_send.at[phase, p], rs_recv.at[phase, p]
        if k == 0:
            term = block(lax.rem(z + 4, NZ)).astype(BF)
            send[0, 0, upper, :] = term[upper.start : upper.start + upper.size]
            send[1, 0, lower, :] = term[lower.start : lower.start + lower.size]
            for copy in rs_copies(p, phase, 0):
                copy.start()
            return
        ahead = block(lax.rem(z + 4 - k, NZ))
        behind = block(lax.rem(z + 4 + k, NZ))
        go, back = rs_copies(p, phase, k - 1)
        go_next, back_next = rs_copies(p, phase, k)
        go.wait_recv()
        if k == 1:
            n = upper.size
            send[0, k, upper, :] = (ahead[:n] + recv[0, 0, upper, :].astype(F32)).astype(BF)
            send[0, k, lower, :] = ahead[n:].astype(BF)
        else:
            send[0, k] = (ahead + recv[0, k - 1].astype(F32)).astype(BF)
        go_next.start()
        back.wait_recv()
        if k == 1:
            send[1, k, upper, :] = behind[:n].astype(BF)
            send[1, k, lower, :] = (behind[n:] + recv[1, 0, lower, :].astype(F32)).astype(BF)
        else:
            send[1, k] = (behind + recv[1, k - 1].astype(F32)).astype(BF)
        back_next.start()

    def rs_end(p, phase, block):
        own = block(z)
        go, back = rs_copies(p, phase, 3)
        go.wait_recv()
        back.wait_recv()
        recv = rs_recv.at[phase, p]
        return own + recv[0, 3].astype(F32) + recv[1, 3].astype(F32)

    def rs_drain(p, phase):
        for k in range(4):
            for copy in rs_copies(p, phase, k):
                copy.wait_send()

    def out_block(p):
        def block(f):
            lanes = pl.ds(pl.multiple_of(f * FB, FB), FB)
            return jnp.dot(
                attended[p * R : (p + 1) * R, :], wout[:, lanes], preferred_element_type=F32
            )

        return block

    def down_block(p):
        def block(f):
            lanes = pl.ds(pl.multiple_of(f * FB, FB), FB)
            return jnp.dot(
                hidden[p * R : (p + 1) * R, :], wdown[:, lanes], preferred_element_type=F32
            )

        return block

    def mix(p):
        rows = pl.ds(p * R, R)
        summed = rs_end(p, 0, out_block(p))
        mixed_all[p, z] = (own_stream[rows, :].astype(F32) + summed).astype(BF)

    def up_part(p, f, own=False):
        rows = pl.ds(p * R, R)
        wide = mixed_all[p, f].astype(F32)
        square = wide * wide
        square = square[:, :128] + square[:, 128:]
        lanes = pl.ds(pl.multiple_of(f * FB, FB), FB)
        normed = (wide * gain2_ref[:, lanes]).astype(BF)
        piece = jnp.dot(normed, wup[lanes, :], preferred_element_type=F32)
        if own:
            acc2[rows, :] = piece
            ssq2[rows, :] = square
        else:
            acc2[rows, :] += piece
            ssq2[rows, :] += square

    def activate(p):
        rows = pl.ds(p * R, R)
        total = jnp.sum(ssq2[rows, :], axis=1, keepdims=True)
        scale = lax.rsqrt(total * (1.0 / D) + 1e-6)
        hidden[rows, :] = jax.nn.gelu(acc2[rows, :] * scale, approximate=True).astype(BF)

    def last(p):
        rows = pl.ds(p * R, R)
        summed = rs_end(p, 1, down_block(p))
        out_ref[rows, :] = (mixed_all[p, z].astype(F32) + summed).astype(BF)

    weights[0].wait()
    for p in range(PARTS):
        embed_block(p, z, own=True)
    for k in range(4):
        ag_wait(*emb_args, k)
        if k < 3:
            ag_start(*emb_args, k + 1)
        for p in range(PARTS):
            ag_wait(*pos_args[p], k)
            if k < 3:
                ag_start(*pos_args[p], k + 1)
            embed_block(p, lax.rem(z + NZ - 1 - k, NZ))
            if k < 3:
                embed_block(p, lax.rem(z + 1 + k, NZ))
    for p in range(PARTS):
        project(p)
        exchange_start(p)
    for p in range(PARTS):
        exchange_wait(p, True, True)
    for p in range(PARTS):
        attend(p)
        give_start(p)
    weights[1].wait()
    for p in range(PARTS):
        give_wait(p)
        combine(p)
    for k in range(4):
        for p in range(PARTS):
            rs_step(p, 0, out_block(p), k)
    weights[2].wait()
    weights[3].wait()
    for p in range(PARTS):
        mix(p)
        ag_start(*mix_args[p], 0)
        up_part(p, z, own=True)
    for k in range(4):
        for p in range(PARTS):
            ag_wait(*mix_args[p], k)
            if k < 3:
                ag_start(*mix_args[p], k + 1)
            up_part(p, lax.rem(z + NZ - 1 - k, NZ))
            if k < 3:
                up_part(p, lax.rem(z + 1 + k, NZ))
    for p in range(PARTS):
        activate(p)
    for k in range(4):
        for p in range(PARTS):
            rs_step(p, 1, down_block(p), k)
    for p in range(PARTS):
        last(p)

    for copy in along_y + along_x + [across]:
        copy.wait_send()
    ag_drain(*emb_args)
    for p in range(PARTS):
        ag_drain(*pos_args[p])
        exchange_drain(p)
        give_drain(p)
        rs_drain(p, 0)
        ag_drain(*mix_args[p])
        rs_drain(p, 1)


def pool_cells(latent):
    pixels = latent.reshape(2, 64, 2, C).astype(jnp.float32)
    pooled = (pixels[0, :, 0] + pixels[0, :, 1] + pixels[1, :, 0] + pixels[1, :, 1]) * 0.25
    high = lax.reduce_precision(pooled, 8, 7)
    mid = lax.reduce_precision(pooled - high, 8, 7)
    low = pooled - high - mid
    return jnp.concatenate([high, mid, low, jnp.zeros_like(low)], axis=1).astype(BF)


def body(latent, pos, embed, gain1, qkv_w, out_w, gain2, up, down):
    vmem = pl.BlockSpec(memory_space=pltpu.VMEM)
    hbm = pl.BlockSpec(memory_space=pl.ANY)
    dma = pltpu.SemaphoreType.DMA
    return pl.pallas_call(
        kernel,
        out_shape=jax.ShapeDtypeStruct((TOK, FB), BF),
        in_specs=[vmem, hbm, hbm, vmem, hbm, hbm, vmem, hbm, hbm],
        out_specs=vmem,
        scratch_shapes=[
            pltpu.VMEM((3, D, FB), BF),
            pltpu.VMEM((FB, D), BF),
            pltpu.VMEM((D, HID), BF),
            pltpu.VMEM((HID, D), BF),
            pltpu.VMEM((2, 4, 4, 64, 128), BF),
            pltpu.VMEM((PARTS, NZ, R, FB), BF),
            pltpu.VMEM((NZ, C, FB), BF),
            pltpu.VMEM((3, TOK, C), BF),
            pltpu.VMEM((TOK, FB), BF),
            pltpu.VMEM((TOK, 3 * FB), F32),
            pltpu.VMEM((TOK, 128), F32),
            pltpu.VMEM((2, TOK, 2 * HS), BF),
            pltpu.VMEM((2, TOK, HS), BF),
            pltpu.VMEM((KEYS, 2 * HS), BF),
            pltpu.VMEM((PARTS, 8, R, HS), BF),
            pltpu.VMEM((PARTS, 8, MSG, HS), BF),
            pltpu.VMEM((PARTS, 8, MSG, HS), BF),
            pltpu.VMEM((2 * R, 2 * HS), F32),
            pltpu.VMEM((2 * R, 128), F32),
            pltpu.VMEM((TOK, FB), BF),
            pltpu.VMEM((2, PARTS, 2, 4, R, FB), BF),
            pltpu.VMEM((2, PARTS, 2, 4, R, FB), BF),
            pltpu.VMEM((PARTS, NZ, R, FB), BF),
            pltpu.VMEM((TOK, HID), F32),
            pltpu.VMEM((TOK, 128), F32),
            pltpu.VMEM((TOK, HID), BF),
            dma((PARTS + 5,)),
            dma((7, 2)),
            dma((PARTS, 2, 4, 2)),
            dma((2, 4, 2)),
            dma((PARTS, 7)),
            dma((PARTS, 8)),
            dma((PARTS, 7)),
            dma((PARTS, 8)),
            dma((PARTS, 7)),
            dma((PARTS, 8)),
            dma((2, PARTS, 2, 4, 2)),
            dma((PARTS, 2, 4, 2)),
        ],
        compiler_params=pltpu.CompilerParams(
            collective_id=0, has_side_effects=True, vmem_limit_bytes=56 * 2**20
        ),
    )(
        pool_cells(latent),
        pos,
        embed,
        gain1.reshape(1, D),
        qkv_w,
        out_w,
        gain2.reshape(1, D),
        up,
        down,
    )


def solution(mesh):
    in_specs = (
        P("seq", None),
        P("seq", "head"),
        P(None, "head"),
        P(),
        P(None, None, "head"),
        P("head", None),
        P(),
        P(None, "head"),
        P("head", None),
    )
    return jax.shard_map(
        body, mesh=mesh, in_specs=in_specs, out_specs=P("seq", "head"), check_vma=False
    )
```

time: 363 us -> 145 us (0.40)
  the two profiles are of different devices: /device:TPU:6 before, /device:TPU:36 now
where the time goes in v1:
time: 145 us; the launch traced here: 144 us
  Pallas kernels  141 us (97%)
  local copies, waits for them, and re-layouts  2.66 us (2%)
    pallas_call x1, Pallas kernels, body(): pl.pallas_call(kernel, out_shape=jax.ShapeDtypeStruct((TOK, FB), BF), in_...  141 us

profile of v1, /device:TPU:36, one launch (start us, length us, event | category | flops | bytes accessed | tf_op | source)
XLA Modules:
  0.0 144.4 jit_solution(6748940591927635941)
XLA Ops:
  0.0 0.1 pad.3.clone
  0.1 0.9 reshape.16
  1.0 0.1 fusion.1
  1.1 0.7 maximum_maximum_fusion.cells_ref
  1.8 140.9 %shard_map.91 = bf16[336,256]{1,0:T(8,128)(2,1)} custom-call(bf16[64,128]{1,0:T(8,128)(2,1)} %maximum_maximum_fusion.cells_ref, bf16[336,256]{1,0:T(8,128)(2,1)} %pos_hbm.1, bf16[32,256]{1,0:T(8,128)(2,1)} %embed_hbm.1, f32[1,2048]{1,0:T(1,128)} %bitcast.17, bf16[3,2048,256]{2,1,0:T(8,128)(2,1)} %qkv_hbm.1, bf16[256,2048]{1,0:T(8,128)(2,1)} %out_w_hbm.1, ...), custom_call_target="tpu_custom_call" | custom-call | tf_op jit(solution)/shard_map/pallas_call | solution.py:701
  142.8 1.6 %copy.19 = bf16[336,256]{1,0:T(8,128)(2,1)} copy(bf16[336,256]{1,0:T(8,128)(2,1)} %shard_map.91) | data formatting | bytes 344064
  (3 shorter events, 0.0 us)

commit v2 on v1

v2 whole, which is shorter than its diff:
```python
import functools

import jax
import jax.numpy as jnp
from jax import lax
from jax.experimental import pallas as pl
from jax.experimental.pallas import tpu as pltpu
from jax.sharding import PartitionSpec as P

D = 2048
HS = 128
C = 32
TOK = 336
FB = 256
HID = 512
FIRST = 512
SECOND = 2560
PARTS = 3
R = TOK // PARTS
MSG = R + 16
NZ = 8
KEYS = 8 * TOK
NEG = -1e30
QSCALE = 1.4426950408889634 / HS**0.5
MESH = pl.DeviceIdType.MESH
BF = jnp.bfloat16
F32 = jnp.float32
NT = (((1,), (1,)), ((), ()))


def split3(wide):
    high = wide.astype(BF)
    rest = wide - high.astype(F32)
    mid = rest.astype(BF)
    low = (rest - mid.astype(F32)).astype(BF)
    return high, mid, low


def level(token):
    return (token >= FIRST).astype(jnp.int32) + (token >= SECOND).astype(jnp.int32)


def halves(rows, p):
    first = ((rows // 16 + p % 2) // 2) * 16
    return pl.ds(0, first), pl.ds(first, rows - first)


def kernel(
    latent_ref,
    pos_hbm,
    embed_hbm,
    gain1_ref,
    qkv_hbm,
    out_w_hbm,
    gain2_ref,
    up_hbm,
    down_hbm,
    out_ref,
    wqkv,
    wout,
    wup,
    wdown,
    grid_cells,
    pos_all,
    emb_all,
    select,
    lines_buf,
    inp,
    own_stream,
    acc,
    ssq,
    kv_send,
    q_send,
    kv_buf,
    q_buf,
    o_send,
    o_recv,
    state_o,
    state_m,
    attended,
    rs_send,
    rs_recv,
    mixed_all,
    acc2,
    ssq2,
    hidden,
    local_sem,
    cell_ssem,
    cell_rsem,
    pos_sem,
    emb_sem,
    kv_ssem,
    kv_rsem,
    q_ssem,
    q_rsem,
    o_ssem,
    o_rsem,
    rs_sem,
    mix_sem,
):
    seq = lax.axis_index("seq")
    z = lax.axis_index("head")
    x, y, c = seq >> 3, (seq >> 1) & 3, seq & 1
    right, left = (z + 1) & 7, (z + 7) & 7
    a0 = jnp.where(c == 0, x, y)
    b0 = jnp.where(c == 0, y, x)

    def sid(px, py, pc):
        return (px * 4 + py) * 2 + pc

    def ring(value, step):
        return (value + step) & 3

    sibling = sid(x, y, 1 - c)

    loads = [
        pltpu.make_async_copy(pos_hbm, pos_all.at[z], local_sem.at[0])
    ]
    loads.append(pltpu.make_async_copy(embed_hbm, emb_all.at[z], local_sem.at[1]))
    weights = [
        pltpu.make_async_copy(src, dst, local_sem.at[2 + i])
        for i, (src, dst) in enumerate(
            ((qkv_hbm, wqkv), (out_w_hbm, wout), (up_hbm, wup), (down_hbm, wdown))
        )
    ]
    for load in loads:
        load.start()
    for load in weights:
        load.start()

    wide = latent_ref[...].astype(F32)
    both = wide[0:1] + wide[1:2]
    for j in range(32):
        lines_buf[j : j + 1, :] = both[:, j * 128 : (j + 1) * 128]
    wide = lines_buf[...] * 0.25
    pooled = jnp.concatenate(
        [wide[:, 0:C] + wide[:, C : 2 * C], wide[:, 2 * C : 3 * C] + wide[:, 3 * C :]], axis=0
    )
    grid_cells[...] = jnp.zeros((32, 64, 128), BF)
    grid_cells[seq] = jnp.concatenate([*split3(pooled), jnp.zeros((64, C), BF)], axis=1)

    token = seq * TOK + lax.broadcasted_iota(jnp.int32, (TOK, 1), 0)
    top, mid_level = token >= SECOND, token >= FIRST
    from_top, from_mid = token - SECOND, token - FIRST
    key_top = (from_top >> 8) * 64 + ((from_top & 127) >> 1)
    key_mid = (from_mid >> 7) * 32 + ((from_mid & 63) >> 1)
    fine_key = jnp.where(top, key_top, -1)
    coarse_key = jnp.where(top, -1, jnp.where(mid_level, key_mid, token))
    col = lax.broadcasted_iota(jnp.int32, (1, 2048), 1)
    cell_row, cell_col = col >> 6, (col & 31) * 2 + ((col >> 5) & 1)
    fine_col = cell_row * 64 + cell_col
    coarse_col = (cell_row >> 1) * 32 + (cell_col >> 1)
    select[...] = jnp.where(
        fine_key == fine_col, 1.0, jnp.where(coarse_key == coarse_col, 0.25, 0.0)
    ).astype(BF)

    barrier = pltpu.get_barrier_semaphore()
    pl.semaphore_signal(barrier, inc=1, device_id={"head": right}, device_id_type=MESH)
    pl.semaphore_signal(barrier, inc=1, device_id={"head": left}, device_id_type=MESH)
    for step in range(1, 32):
        peer = (seq + step) & 31
        pl.semaphore_signal(barrier, inc=1, device_id={"seq": peer}, device_id_type=MESH)
    pl.semaphore_wait(barrier, 33)

    def remote(src, dst, ssem, rsem, **where):
        return pltpu.make_async_remote_copy(
            src_ref=src,
            dst_ref=dst,
            send_sem=ssem,
            recv_sem=rsem,
            device_id=where,
            device_id_type=MESH,
        )

    def ag_copies(buf, sems, base, rows, p, k):
        go, back = (z - k) & 7, (z + k) & 7
        if k == 3:
            upper, lower = halves(rows, p)
            upper = pl.ds(base + upper.start, upper.size)
            lower = pl.ds(base + lower.start, lower.size)
        else:
            upper = lower = pl.ds(base, rows)
        return (
            remote(buf.at[go, upper], buf.at[go, upper], sems.at[0, k, 0], sems.at[0, k, 1], head=right),
            remote(buf.at[back, lower], buf.at[back, lower], sems.at[1, k, 0], sems.at[1, k, 1], head=left),
        )

    def ag_start(*args):
        for copy in ag_copies(*args):
            copy.start()

    def ag_wait(*args):
        for copy in ag_copies(*args):
            copy.wait_recv()

    def ag_drain(*args):
        for k in range(4):
            for copy in ag_copies(*args, k):
                copy.wait_send()

    pos_args = [(pos_all, pos_sem.at[p], p * R, R, p) for p in range(PARTS)]
    emb_args = (emb_all, emb_sem, 0, C, 0)
    mix_args = [(mixed_all.at[p], mix_sem.at[p], 0, R, p) for p in range(PARTS)]

    for load in loads:
        load.wait()
    ag_start(*emb_args, 0)
    for p in range(PARTS):
        ag_start(*pos_args[p], 0)

    def takers(row):
        fine, coarse = SECOND + 256 * row, row >> 1
        middle, low = FIRST + 128 * coarse, 32 * coarse
        return (fine, fine + 255), (middle, middle + 127), (low, low + 31)

    def owner(token):
        return (token * 49933) >> 24

    def cell_copy(i, row, dest):
        return remote(
            grid_cells.at[row], grid_cells.at[row], cell_ssem.at[i], cell_rsem.at[row], seq=dest
        )

    def each_taker(act):
        for i, ends in enumerate(takers(seq)):
            one, two = owner(ends[0]), owner(ends[1])

            @pl.when(one != seq)
            def _():
                act(cell_copy(2 * i, seq, one))

            @pl.when(jnp.logical_and(two != one, two != seq))
            def _():
                act(cell_copy(2 * i + 1, seq, two))

    each_taker(lambda copy: copy.start())

    def wait_cells():
        start, end = seq * TOK, seq * TOK + TOK - 1

        def wait_rows(low, high):
            @pl.loop(low, high)
            def _(row):
                @pl.when(row != seq)
                def _():
                    cell_copy(0, row, sibling).wait_recv()

        @pl.when(end >= SECOND)
        def _():
            wait_rows(jnp.maximum(start - SECOND, 0) >> 8, ((end - SECOND) >> 8) + 1)

        @pl.when(jnp.logical_and(end >= FIRST, start < SECOND))
        def _():
            wait_rows(
                (jnp.maximum(start - FIRST, 0) >> 7) * 2,
                ((jnp.minimum(end, SECOND - 1) - FIRST) >> 7) * 2 + 2,
            )

        @pl.when(start < FIRST)
        def _():
            wait_rows((start >> 5) * 2, (jnp.minimum(end, FIRST - 1) >> 5) * 2 + 2)

    def pool_inputs():
        pooled = jnp.dot(
            select[...], grid_cells[...].reshape(2048, 128), preferred_element_type=F32
        )
        inputs = pooled[:, 0:C] + pooled[:, C : 2 * C] + pooled[:, 2 * C : 3 * C]
        for i, piece in enumerate(split3(inputs)):
            inp[i] = piece

    def group_rows(p):
        return pl.ds(p * R, R)

    def embed_block(g, f, own=False):
        rows = group_rows(g)
        emb = emb_all[f]
        wide = pos_all[f, rows, :].astype(F32)
        for i in range(3):
            wide = wide + jnp.dot(inp[i, rows, :], emb, preferred_element_type=F32)
        stream = wide.astype(BF)
        if own:
            own_stream[rows, :] = stream
        wide = stream.astype(F32)
        square = wide * wide
        square = square[:, :128] + square[:, 128:]
        lanes = pl.ds(pl.multiple_of(f * FB, FB), FB)
        normed = (wide * gain1_ref[:, lanes]).astype(BF)
        for j in range(3):
            piece = jnp.dot(normed, wqkv[j, lanes, :], preferred_element_type=F32)
            if own:
                acc[rows, j * FB : (j + 1) * FB] = piece
            else:
                acc[rows, j * FB : (j + 1) * FB] += piece
        if own:
            ssq[rows, :] = square
        else:
            ssq[rows, :] += square

    def project(g):
        rows = group_rows(g)
        total = jnp.sum(ssq[rows, :], axis=1, keepdims=True)
        scale = lax.rsqrt(total * (1.0 / D) + 1e-6)
        for h in range(2):
            cols = slice(h * HS, (h + 1) * HS)
            q_send[h, rows, :] = (acc[rows, cols] * (scale * QSCALE)).astype(BF)
            kv_send[h, rows, 0:HS] = (acc[rows, FB + h * HS : FB + (h + 1) * HS] * scale).astype(BF)
            kv_send[h, rows, HS:] = (
                acc[rows, 2 * FB + h * HS : 2 * FB + (h + 1) * HS] * scale
            ).astype(BF)

    def slot_rows(slot, g):
        return pl.ds(pl.multiple_of(slot * TOK + g * R, 16), R)

    def exchange(p):
        rows = group_rows(p)
        kv_copies, q_copies = [], []

        def kv_copy(i, head, slot, dest):
            return remote(
                kv_send.at[head, rows],
                kv_buf.at[slot_rows(slot, p)],
                kv_ssem.at[p, i],
                kv_rsem.at[p, slot],
                seq=dest,
            )

        def q_copy(i, head, slot, dest):
            return remote(
                q_send.at[head, rows],
                q_buf.at[slot_rows(slot, p)],
                q_ssem.at[p, i],
                q_rsem.at[p, slot],
                seq=dest,
            )

        other = 1 - c
        kv_copies.append(kv_copy(6, other, jnp.where(c == 1, x, y) * 2 + c, sibling))
        q_copies.append(q_copy(6, other, jnp.where(c == 1, y, x) * 2 + c, sibling))
        for i, step in enumerate((1, 3, 2)):
            kv_copies.append(kv_copy(i, 0, x * 2 + c, sid(ring(x, step), y, 0)))
            kv_copies.append(kv_copy(3 + i, 1, y * 2 + c, sid(x, ring(y, step), 1)))
            q_copies.append(q_copy(i, 0, y * 2 + c, sid(x, ring(y, step), 0)))
            q_copies.append(q_copy(3 + i, 1, x * 2 + c, sid(ring(x, step), y, 1)))
        return kv_copies, q_copies

    def exchange_start(p):
        rows = group_rows(p)
        kv_copies, q_copies = exchange(p)
        for copy in q_copies + kv_copies:
            copy.start()
        kv_buf[slot_rows(a0 * 2 + c, p), :] = kv_send[c, rows, :]
        q_buf[slot_rows(b0 * 2 + c, p), :] = q_send[c, rows, :]

    def exchange_wait(p, want_q, want_kv):
        rows = group_rows(p)
        for i in range(1, 8):
            if want_q:
                slot = (b0 * 2 + c + i) & 7
                remote(
                    q_send.at[0, rows],
                    q_buf.at[slot_rows(slot, p)],
                    q_ssem.at[p, 0],
                    q_rsem.at[p, slot],
                    seq=sibling,
                ).wait_recv()
            if want_kv:
                slot = (a0 * 2 + c + i) & 7
                remote(
                    kv_send.at[0, rows],
                    kv_buf.at[slot_rows(slot, p)],
                    kv_ssem.at[p, 0],
                    kv_rsem.at[p, slot],
                    seq=sibling,
                ).wait_recv()

    def exchange_drain(p):
        kv_copies, q_copies = exchange(p)
        for copy in q_copies + kv_copies:
            copy.wait_send()

    ones_row = jnp.ones((1, HS), BF)

    def values_and_ones(kv):
        return jnp.concatenate([kv[:, HS:], jnp.broadcast_to(ones_row, (kv.shape[0], HS))], axis=1)

    diag = lax.broadcasted_iota(jnp.int32, (128, 128), 0) == lax.broadcasted_iota(
        jnp.int32, (128, 128), 1
    )

    def finish(slot, total, largest):
        sums = total[:, HS:]
        normal = (total[:, :HS] / sums).astype(BF)
        log_sum = largest + jnp.log2(sums)
        for p in range(PARTS):
            low = p * R
            o_send[p, slot, 0:R, :] = normal[low : low + R]
            tile = jnp.concatenate(
                [log_sum[low : low + R], jnp.zeros((128 - R, 128), F32)], axis=0
            )
            line = jnp.sum(jnp.where(diag, tile, 0.0), axis=0, keepdims=True)
            packed = [v.astype(F32) for v in split3(line)] + [jnp.zeros((13, 128), F32)]
            o_send[p, slot, R:MSG, :] = jnp.concatenate(packed, axis=0).astype(BF)

    CHUNK = 896

    def plain_slot(slot):
        queries = q_buf[pl.ds(pl.multiple_of(slot * TOK, 16), TOK), :]
        largest = total = None
        for low in range(0, KEYS, CHUNK):
            kv = kv_buf[low : low + CHUNK, :]
            scores = lax.dot_general(queries, kv[:, :HS], NT, preferred_element_type=F32)
            newest = jnp.max(scores, axis=1, keepdims=True)
            if total is not None:
                newest = jnp.maximum(newest, largest)
            weights = jnp.exp2(scores - newest).astype(BF)
            part = jnp.dot(weights, values_and_ones(kv), preferred_element_type=F32)
            total = part if total is None else total * jnp.exp2(largest - newest) + part
            largest = newest
        finish(slot, total, largest)

    def masked_slot(slot, chunks):
        b, core = slot >> 1, slot & 1
        first_q = jnp.where(c == 0, x * 8 + b * 2, b * 8 + y * 2) + core
        q_level = level(first_q * TOK + lax.broadcasted_iota(jnp.int32, (TOK, 1), 0))
        state_m[...] = jnp.full((TOK, 128), NEG, F32)
        state_o[...] = jnp.zeros((TOK, 2 * HS), F32)

        @pl.loop(0, chunks)
        def _(i):
            low = pl.multiple_of(i * CHUNK, 128)
            kv = kv_buf[pl.ds(low, CHUNK), :]
            queries = q_buf[pl.ds(pl.multiple_of(slot * TOK, 16), TOK), :]
            scores = lax.dot_general(queries, kv[:, :HS], NT, preferred_element_type=F32)
            key = low + lax.broadcasted_iota(jnp.int32, (1, CHUNK), 1)
            block = sum((key >= edge * 2 * TOK).astype(jnp.int32) for edge in (1, 2, 3))
            shift = jnp.where(c == 0, block * (6 * TOK) + y * 2 * TOK, x * 8 * TOK)
            scores = jnp.where(level(key + shift) <= q_level, scores, NEG)
            before = state_m[:, 0:1]
            newest = jnp.maximum(before, jnp.max(scores, axis=1, keepdims=True))
            weights = jnp.exp2(scores - newest).astype(BF)
            part = jnp.dot(weights, values_and_ones(kv), preferred_element_type=F32)
            state_o[...] = state_o[...] * jnp.exp2(before - newest) + part
            state_m[...] = jnp.broadcast_to(newest, (TOK, 128))

        finish(slot, state_o[...], state_m[:, 0:1])

    def attend():
        first_plain = jnp.where(c == 0, jnp.where(x == 0, 4, 0), 1)

        @pl.loop(first_plain, 4)
        def _(b):
            plain_slot(b * 2)
            plain_slot(b * 2 + 1)

        nothing = jnp.logical_and(c == 1, jnp.logical_and(x >= 1, y < 3))

        @pl.when(nothing)
        def _():
            for i in range(2):
                for p in range(PARTS):
                    o_send[p, i, 0:R, :] = jnp.zeros((R, HS), BF)
                    o_send[p, i, R:MSG, :] = jnp.full((MSG - R, HS), NEG, BF)

        @pl.when(jnp.logical_not(nothing))
        def _():
            @pl.loop(0, first_plain * 2)
            def _(slot):
                masked_slot(slot, jnp.where(jnp.logical_and(c == 0, slot < 7), 1, 3))

    def give_copies(p):
        copies = [
            remote(
                o_send.at[p, b0 * 2 + 1 - c],
                o_recv.at[p, c * 4 + b0],
                o_ssem.at[p, 6],
                o_rsem.at[p, c * 4 + b0],
                seq=sibling,
            )
        ]
        for i, step in enumerate((1, 3, 2)):
            b = ring(b0, step)
            for core in (0, 1):
                dest = jnp.where(c == 0, sid(x, b, core), sid(b, y, core))
                copies.append(
                    remote(
                        o_send.at[p, b * 2 + core],
                        o_recv.at[p, c * 4 + b0],
                        o_ssem.at[p, i * 2 + core],
                        o_rsem.at[p, c * 4 + b0],
                        seq=dest,
                    )
                )
        return copies

    def give_start(p):
        for copy in give_copies(p):
            copy.start()
        o_recv[p, c * 4 + b0] = o_send[p, b0 * 2 + c]

    def give_wait(p):
        for i in range(1, 8):
            slot = (c * 4 + b0 + i) & 7
            remote(
                o_send.at[p, 0],
                o_recv.at[p, slot],
                o_ssem.at[p, 0],
                o_rsem.at[p, slot],
                seq=sibling,
            ).wait_recv()

    def give_drain(p):
        for copy in give_copies(p):
            copy.wait_send()

    def combine(p):
        tails = [o_recv[p, i, R:MSG, :].astype(F32) for i in range(8)]
        logs = [t[0:1] + t[1:2] + t[2:3] for t in tails]
        for h in range(2):
            four = logs[h * 4 : h * 4 + 4]
            largest = functools.reduce(jnp.maximum, four)
            powers = [jnp.exp2(v - largest) for v in four]
            total = powers[0] + powers[1] + powers[2] + powers[3]
            mean = None
            for a in range(4):
                share = jnp.sum(
                    jnp.where(diag, powers[a] / total, 0.0), axis=1, keepdims=True
                )
                term = o_recv[p, h * 4 + a, 0:R, :].astype(F32) * share[:R]
                mean = term if mean is None else mean + term
            attended[p * R : (p + 1) * R, h * HS : (h + 1) * HS] = mean.astype(BF)

    def rs_copies(p, phase, k):
        upper, lower = halves(R, p)
        if k > 0:
            upper = lower = pl.ds(0, R)
        send, recv, sems = rs_send.at[phase, p], rs_recv.at[phase, p], rs_sem.at[phase, p]
        return (
            remote(send.at[0, k, upper], recv.at[0, k, upper], sems.at[0, k, 0], sems.at[0, k, 1], head=right),
            remote(send.at[1, k, lower], recv.at[1, k, lower], sems.at[1, k, 0], sems.at[1, k, 1], head=left),
        )

    def rs_step(p, phase, block, k):
        upper, lower = halves(R, p)
        send, recv = rs_send.at[phase, p], rs_recv.at[phase, p]
        if k == 0:
            term = block((z + 4) & 7).astype(BF)
            send[0, 0, upper, :] = term[upper.start : upper.start + upper.size]
            send[1, 0, lower, :] = term[lower.start : lower.start + lower.size]
            for copy in rs_copies(p, phase, 0):
                copy.start()
            return
        ahead = block((z + 4 - k) & 7)
        behind = block((z + 4 + k) & 7)
        go, back = rs_copies(p, phase, k - 1)
        go_next, back_next = rs_copies(p, phase, k)
        go.wait_recv()
        if k == 1:
            n = upper.size
            send[0, k, upper, :] = (ahead[:n] + recv[0, 0, upper, :].astype(F32)).astype(BF)
            send[0, k, lower, :] = ahead[n:].astype(BF)
        else:
            send[0, k] = (ahead + recv[0, k - 1].astype(F32)).astype(BF)
        go_next.start()
        back.wait_recv()
        if k == 1:
            send[1, k, upper, :] = behind[:n].astype(BF)
            send[1, k, lower, :] = (behind[n:] + recv[1, 0, lower, :].astype(F32)).astype(BF)
        else:
            send[1, k] = (behind + recv[1, k - 1].astype(F32)).astype(BF)
        back_next.start()

    def rs_end(p, phase, block):
        own = block(z)
        go, back = rs_copies(p, phase, 3)
        go.wait_recv()
        back.wait_recv()
        recv = rs_recv.at[phase, p]
        return own + recv[0, 3].astype(F32) + recv[1, 3].astype(F32)

    def rs_drain(p, phase):
        for k in range(4):
            for copy in rs_copies(p, phase, k):
                copy.wait_send()

    def out_block(p):
        def block(f):
            lanes = pl.ds(pl.multiple_of(f * FB, FB), FB)
            return jnp.dot(
                attended[p * R : (p + 1) * R, :], wout[:, lanes], preferred_element_type=F32
            )

        return block

    def down_block(p):
        def block(f):
            lanes = pl.ds(pl.multiple_of(f * FB, FB), FB)
            return jnp.dot(
                hidden[p * R : (p + 1) * R, :], wdown[:, lanes], preferred_element_type=F32
            )

        return block

    def mix(p):
        rows = pl.ds(p * R, R)
        summed = rs_end(p, 0, out_block(p))
        mixed_all[p, z] = (own_stream[rows, :].astype(F32) + summed).astype(BF)

    def up_part(p, f, own=False):
        rows = pl.ds(p * R, R)
        wide = mixed_all[p, f].astype(F32)
        square = wide * wide
        square = square[:, :128] + square[:, 128:]
        lanes = pl.ds(pl.multiple_of(f * FB, FB), FB)
        normed = (wide * gain2_ref[:, lanes]).astype(BF)
        piece = jnp.dot(normed, wup[lanes, :], preferred_element_type=F32)
        if own:
            acc2[rows, :] = piece
            ssq2[rows, :] = square
        else:
            acc2[rows, :] += piece
            ssq2[rows, :] += square

    def activate(p):
        rows = pl.ds(p * R, R)
        total = jnp.sum(ssq2[rows, :], axis=1, keepdims=True)
        scale = lax.rsqrt(total * (1.0 / D) + 1e-6)
        hidden[rows, :] = jax.nn.gelu(acc2[rows, :] * scale, approximate=True).astype(BF)

    def last(p):
        rows = pl.ds(p * R, R)
        summed = rs_end(p, 1, down_block(p))
        out_ref[rows, :] = (mixed_all[p, z].astype(F32) + summed).astype(BF)

    def embed_work(g, k):
        embed_block(g, (z - 1 - k) & 7)
        if k < 3:
            embed_block(g, (z + 1 + k) & 7)

    def chain(p):
        give_wait(p)
        combine(p)
        for k in range(4):
            rs_step(p, 0, out_block(p), k)
            yield
        mix(p)
        ag_start(*mix_args[p], 0)
        up_part(p, z, own=True)
        yield
        for k in range(4):
            ag_wait(*mix_args[p], k)
            if k < 3:
                ag_start(*mix_args[p], k + 1)
            up_part(p, (z - 1 - k) & 7)
            if k < 3:
                up_part(p, (z + 1 + k) & 7)
                yield
        activate(p)
        for k in range(4):
            rs_step(p, 1, down_block(p), k)
            yield
        last(p)
        yield

    for k in range(4):
        ag_wait(*emb_args, k)
        if k < 3:
            ag_start(*emb_args, k + 1)
        for p in range(PARTS):
            ag_wait(*pos_args[p], k)
            if k < 3:
                ag_start(*pos_args[p], k + 1)
            if k > 0:
                embed_work(p, k - 1)
            if k == 3:
                embed_work(p, k)
                project(p)
                exchange_start(p)
        if k == 0:
            wait_cells()
            pool_inputs()
            weights[0].wait()
            for p in range(PARTS):
                embed_block(p, z, own=True)
    for i in range(1, 4):
        weights[i].wait()
    for p in range(PARTS):
        exchange_wait(p, True, True)
    attend()
    for p in range(PARTS):
        give_start(p)
    chains = [chain(p) for p in range(PARTS)]
    while chains:
        for each in list(chains):
            if next(each, 0) == 0:
                chains.remove(each)

    each_taker(lambda copy: copy.wait_send())
    ag_drain(*emb_args)
    for g in range(PARTS):
        exchange_drain(g)
    for p in range(PARTS):
        ag_drain(*pos_args[p])
        give_drain(p)
        rs_drain(p, 0)
        ag_drain(*mix_args[p])
        rs_drain(p, 1)


def body(latent, pos, embed, gain1, qkv_w, out_w, gain2, up, down):
    vmem = pl.BlockSpec(memory_space=pltpu.VMEM)
    hbm = pl.BlockSpec(memory_space=pl.ANY)
    dma = pltpu.SemaphoreType.DMA
    return pl.pallas_call(
        kernel,
        out_shape=jax.ShapeDtypeStruct((TOK, FB), BF),
        in_specs=[vmem, hbm, hbm, vmem, hbm, hbm, vmem, hbm, hbm],
        out_specs=vmem,
        scratch_shapes=[
            pltpu.VMEM((3, D, FB), BF),
            pltpu.VMEM((FB, D), BF),
            pltpu.VMEM((D, HID), BF),
            pltpu.VMEM((HID, D), BF),
            pltpu.VMEM((32, 64, 128), BF),
            pltpu.VMEM((NZ, TOK, FB), BF),
            pltpu.VMEM((NZ, C, FB), BF),
            pltpu.VMEM((TOK, 2048), BF),
            pltpu.VMEM((32, 128), F32),
            pltpu.VMEM((3, TOK, C), BF),
            pltpu.VMEM((TOK, FB), BF),
            pltpu.VMEM((TOK, 3 * FB), F32),
            pltpu.VMEM((TOK, 128), F32),
            pltpu.VMEM((2, TOK, 2 * HS), BF),
            pltpu.VMEM((2, TOK, HS), BF),
            pltpu.VMEM((KEYS, 2 * HS), BF),
            pltpu.VMEM((KEYS, HS), BF),
            pltpu.VMEM((PARTS, 8, MSG, HS), BF),
            pltpu.VMEM((PARTS, 8, MSG, HS), BF),
            pltpu.VMEM((TOK, 2 * HS), F32),
            pltpu.VMEM((TOK, 128), F32),
            pltpu.VMEM((TOK, FB), BF),
            pltpu.VMEM((2, PARTS, 2, 4, R, FB), BF),
            pltpu.VMEM((2, PARTS, 2, 4, R, FB), BF),
            pltpu.VMEM((PARTS, NZ, R, FB), BF),
            pltpu.VMEM((TOK, HID), F32),
            pltpu.VMEM((TOK, 128), F32),
            pltpu.VMEM((TOK, HID), BF),
            dma((6,)),
            dma((6,)),
            dma((32,)),
            dma((PARTS, 2, 4, 2)),
            dma((2, 4, 2)),
            dma((PARTS, 7)),
            dma((PARTS, 8)),
            dma((PARTS, 7)),
            dma((PARTS, 8)),
            dma((PARTS, 7)),
            dma((PARTS, 8)),
            dma((2, PARTS, 2, 4, 2)),
            dma((PARTS, 2, 4, 2)),
        ],
        compiler_params=pltpu.CompilerParams(
            collective_id=0, has_side_effects=True, vmem_limit_bytes=56 * 2**20
        ),
    )(
        latent,
        pos,
        embed,
        gain1.reshape(1, D),
        qkv_w,
        out_w,
        gain2.reshape(1, D),
        up,
        down,
    )


def solution(mesh):
    in_specs = (
        P("seq", None),
        P("seq", "head"),
        P(None, "head"),
        P(),
        P(None, None, "head"),
        P("head", None),
        P(),
        P(None, "head"),
        P("head", None),
    )
    return jax.shard_map(
        body, mesh=mesh, in_specs=in_specs, out_specs=P("seq", "head"), check_vma=False
    )
```

time: 145 us -> 115 us (0.79)
  the two profiles are of different devices: /device:TPU:36 before, /device:TPU:6 now
where the time goes in v2:
time: 115 us; the launch traced here: 114 us
  Pallas kernels  113 us (98%)
  local copies, waits for them, and re-layouts  1.6 us (1%)
    pallas_call x1, Pallas kernels, body(): pl.pallas_call(kernel, out_shape=jax.ShapeDtypeStruct((TOK, FB), BF), in_...  113 us

profile of v2, /device:TPU:6, one launch (start us, length us, event | category | flops | bytes accessed | tf_op | source)
XLA Modules:
  0.0 114.4 jit_solution(16233004510312959572)
XLA Ops:
  0.0 112.8 %shard_map.91 = bf16[336,256]{1,0:T(8,128)(2,1)} custom-call(bf16[2,4096]{1,0:T(2,128)(2,1)} %latent_ref.1, bf16[336,256]{1,0:T(8,128)(2,1)} %pos_hbm.1, bf16[32,256]{1,0:T(8,128)(2,1)} %embed_hbm.1, f32[1,2048]{1,0:T(1,128)} %bitcast.2, bf16[3,2048,256]{2,1,0:T(8,128)(2,1)} %qkv_hbm.1, bf16[256,2048]{1,0:T(8,128)(2,1)} %out_w_hbm.1, f32[1,2048]{1,0:T(1,128)} %bitcast.3, ...), custom_call_target="tpu_custom_call" | custom-call | tf_op jit(solution)/shard_map/pallas_call | solution.py:713
  112.8 1.6 %copy.11 = bf16[336,256]{1,0:T(8,128)(2,1)} copy(bf16[336,256]{1,0:T(8,128)(2,1)} %shard_map.91) | data formatting | bytes 344064

commit v3 on v2

--- a/solution.py
+++ b/solution.py
@@ -418,40 +418,72 @@
             largest = newest
         finish(slot, total, largest)
 
-    def masked_slot(slot, chunks):
-        b, core = slot >> 1, slot & 1
-        first_q = jnp.where(c == 0, x * 8 + b * 2, b * 8 + y * 2) + core
-        q_level = level(first_q * TOK + lax.broadcasted_iota(jnp.int32, (TOK, 1), 0))
-        state_m[...] = jnp.full((TOK, 128), NEG, F32)
-        state_o[...] = jnp.zeros((TOK, 2 * HS), F32)
+    def masked_block(b, chunks):
+        first_q = jnp.where(c == 0, x * 8 + b * 2, b * 8 + y * 2)
+        state_m[...] = jnp.full((2, TOK, 128), NEG, F32)
+        state_o[...] = jnp.zeros((2, TOK, 2 * HS), F32)
 
         @pl.loop(0, chunks)
         def _(i):
             low = pl.multiple_of(i * CHUNK, 128)
             kv = kv_buf[pl.ds(low, CHUNK), :]
-            queries = q_buf[pl.ds(pl.multiple_of(slot * TOK, 16), TOK), :]
-            scores = lax.dot_general(queries, kv[:, :HS], NT, preferred_element_type=F32)
             key = low + lax.broadcasted_iota(jnp.int32, (1, CHUNK), 1)
             block = sum((key >= edge * 2 * TOK).astype(jnp.int32) for edge in (1, 2, 3))
             shift = jnp.where(c == 0, block * (6 * TOK) + y * 2 * TOK, x * 8 * TOK)
-            scores = jnp.where(level(key + shift) <= q_level, scores, NEG)
-            before = state_m[:, 0:1]
-            newest = jnp.maximum(before, jnp.max(scores, axis=1, keepdims=True))
-            weights = jnp.exp2(scores - newest).astype(BF)
-            part = jnp.dot(weights, values_and_ones(kv), preferred_element_type=F32)
-            state_o[...] = state_o[...] * jnp.exp2(before - newest) + part
-            state_m[...] = jnp.broadcast_to(newest, (TOK, 128))
-
-        finish(slot, state_o[...], state_m[:, 0:1])
+            k_level = level(key + shift)
+            for core in range(2):
+                row = pl.multiple_of((b * 2 + core) * TOK, 16)
+                queries = q_buf[pl.ds(row, TOK), :]
+                scores = lax.dot_general(queries, kv[:, :HS], NT, preferred_element_type=F32)
+                token = (first_q + core) * TOK + lax.broadcasted_iota(jnp.int32, (TOK, 1), 0)
+                scores = jnp.where(k_level <= level(token), scores, NEG)
+                before = state_m[core, :, 0:1]
+                newest = jnp.maximum(before, jnp.max(scores, axis=1, keepdims=True))
+                weights = jnp.exp2(scores - newest).astype(BF)
+                part = jnp.dot(weights, values_and_ones(kv), preferred_element_type=F32)
+                state_o[core] = state_o[core] * jnp.exp2(before - newest) + part
+                state_m[core] = jnp.broadcast_to(newest, (TOK, 128))
+
+        @pl.loop(0, 2)
+        def _(core):
+            finish(b * 2 + core, state_o[core], state_m[core, :, 0:1])
+
+    def give_copies(slot, act, keep):
+        b, core = slot >> 1, slot & 1
+        dest = jnp.where(c == 0, sid(x, b, core), sid(b, y, core))
+
+        @pl.when(dest != seq)
+        def _():
+            for p in range(PARTS):
+                act(
+                    remote(
+                        o_send.at[p, slot],
+                        o_recv.at[p, c * 4 + b0],
+                        o_ssem.at[p, slot],
+                        o_rsem.at[p, c * 4 + b0],
+                        seq=dest,
+                    )
+                )
+
+        if keep:
+
+            @pl.when(dest == seq)
+            def _():
+                for p in range(PARTS):
+                    o_recv[p, c * 4 + b0] = o_send[p, slot]
+
+    def give_block(b):
+        @pl.loop(0, 2)
+        def _(core):
+            give_copies(b * 2 + core, lambda copy: copy.start(), True)
+
+    def give_drain():
+        @pl.loop(0, 8)
+        def _(slot):
+            give_copies(slot, lambda copy: copy.wait_send(), False)
 
     def attend():
         first_plain = jnp.where(c == 0, jnp.where(x == 0, 4, 0), 1)
-
-        @pl.loop(first_plain, 4)
-        def _(b):
-            plain_slot(b * 2)
-            plain_slot(b * 2 + 1)
-
         nothing = jnp.logical_and(c == 1, jnp.logical_and(x >= 1, y < 3))
 
         @pl.when(nothing)
@@ -460,42 +492,23 @@
                 for p in range(PARTS):
                     o_send[p, i, 0:R, :] = jnp.zeros((R, HS), BF)
                     o_send[p, i, R:MSG, :] = jnp.full((MSG - R, HS), NEG, BF)
+            give_block(0)
 
         @pl.when(jnp.logical_not(nothing))
         def _():
-            @pl.loop(0, first_plain * 2)
-            def _(slot):
-                masked_slot(slot, jnp.where(jnp.logical_and(c == 0, slot < 7), 1, 3))
-
-    def give_copies(p):
-        copies = [
-            remote(
-                o_send.at[p, b0 * 2 + 1 - c],
-                o_recv.at[p, c * 4 + b0],
-                o_ssem.at[p, 6],
-                o_rsem.at[p, c * 4 + b0],
-                seq=sibling,
-            )
-        ]
-        for i, step in enumerate((1, 3, 2)):
-            b = ring(b0, step)
-            for core in (0, 1):
-                dest = jnp.where(c == 0, sid(x, b, core), sid(b, y, core))
-                copies.append(
-                    remote(
-                        o_send.at[p, b * 2 + core],
-                        o_recv.at[p, c * 4 + b0],
-                        o_ssem.at[p, i * 2 + core],
-                        o_rsem.at[p, c * 4 + b0],
-                        seq=dest,
-                    )
-                )
-        return copies
-
-    def give_start(p):
-        for copy in give_copies(p):
-            copy.start()
-        o_recv[p, c * 4 + b0] = o_send[p, b0 * 2 + c]
+            @pl.loop(0, first_plain)
+            def _(b):
+                masked_block(b, jnp.where(jnp.logical_and(c == 0, b < 3), 1, 3))
+                give_block(b)
+
+        @pl.loop(first_plain, 4)
+        def _(i):
+            turn = b0 + i - first_plain
+            turn = jnp.where(turn >= 3, turn - 3, turn)
+            b = jnp.where(c == 0, (b0 + 1 + i) & 3, 1 + turn)
+            plain_slot(b * 2)
+            plain_slot(b * 2 + 1)
+            give_block(b)
 
     def give_wait(p):
         for i in range(1, 8):
@@ -507,10 +520,6 @@
                 o_rsem.at[p, slot],
                 seq=sibling,
             ).wait_recv()
-
-    def give_drain(p):
-        for copy in give_copies(p):
-            copy.wait_send()
 
     def combine(p):
         tails = [o_recv[p, i, R:MSG, :].astype(F32) for i in range(8)]
@@ -686,8 +695,6 @@
     for p in range(PARTS):
         exchange_wait(p, True, True)
     attend()
-    for p in range(PARTS):
-        give_start(p)
     chains = [chain(p) for p in range(PARTS)]
     while chains:
         for each in list(chains):
@@ -695,12 +702,12 @@
                 chains.remove(each)
 
     each_taker(lambda copy: copy.wait_send())
+    give_drain()
     ag_drain(*emb_args)
     for g in range(PARTS):
         exchange_drain(g)
     for p in range(PARTS):
         ag_drain(*pos_args[p])
-        give_drain(p)
         rs_drain(p, 0)
         ag_drain(*mix_args[p])
         rs_drain(p, 1)
@@ -735,8 +742,8 @@
             pltpu.VMEM((KEYS, HS), BF),
             pltpu.VMEM((PARTS, 8, MSG, HS), BF),
             pltpu.VMEM((PARTS, 8, MSG, HS), BF),
-            pltpu.VMEM((TOK, 2 * HS), F32),
-            pltpu.VMEM((TOK, 128), F32),
+            pltpu.VMEM((2, TOK, 2 * HS), F32),
+            pltpu.VMEM((2, TOK, 128), F32),
             pltpu.VMEM((TOK, FB), BF),
             pltpu.VMEM((2, PARTS, 2, 4, R, FB), BF),
             pltpu.VMEM((2, PARTS, 2, 4, R, FB), BF),
@@ -753,7 +760,7 @@
             dma((PARTS, 8)),
             dma((PARTS, 7)),
             dma((PARTS, 8)),
-            dma((PARTS, 7)),
+            dma((PARTS, 8)),
             dma((PARTS, 8)),
             dma((2, PARTS, 2, 4, 2)),
             dma((PARTS, 2, 4, 2)),

time: 115 us -> 113 us (0.983)
  Pallas kernels: 113 us -> 111 us
    pallas_call x1, Pallas kernels: 113 us -> 111 us  [body(): pl.pallas_call(kernel, out_shape=jax.ShapeDtypeStruct((TOK, FB), BF), in_...]
where the time goes in v3:
time: 113 us
  Pallas kernels  111 us (98%)
  local copies, waits for them, and re-layouts  1.6 us (1%)
    pallas_call x1, Pallas kernels, body(): pl.pallas_call(kernel, out_shape=jax.ShapeDtypeStruct((TOK, FB), BF), in_...  111 us

profile of v3, /device:TPU:6, one launch (start us, length us, event | category | flops | bytes accessed | tf_op | source)
XLA Modules:
  0.0 112.5 jit_solution(15726330400559885214)
XLA Ops:
  0.0 110.9 %shard_map.91 = bf16[336,256]{1,0:T(8,128)(2,1)} custom-call(bf16[2,4096]{1,0:T(2,128)(2,1)} %latent_ref.1, bf16[336,256]{1,0:T(8,128)(2,1)} %pos_hbm.1, bf16[32,256]{1,0:T(8,128)(2,1)} %embed_hbm.1, f32[1,2048]{1,0:T(1,128)} %bitcast.2, bf16[3,2048,256]{2,1,0:T(8,128)(2,1)} %qkv_hbm.1, bf16[256,2048]{1,0:T(8,128)(2,1)} %out_w_hbm.1, f32[1,2048]{1,0:T(1,128)} %bitcast.3, ...), custom_call_target="tpu_custom_call" | custom-call | tf_op jit(solution)/shard_map/pallas_call | solution.py:720
  110.9 1.6 %copy.11 = bf16[336,256]{1,0:T(8,128)(2,1)} copy(bf16[336,256]{1,0:T(8,128)(2,1)} %shard_map.91) | data formatting | bytes 344064

commit v4 on v3

--- a/solution.py
+++ b/solution.py
@@ -189,9 +189,16 @@
         for copy in ag_copies(*args):
             copy.start()
 
-    def ag_wait(*args):
-        for copy in ag_copies(*args):
+    def ag_step(*args):
+        *where, k = args
+        here = ag_copies(*where, k)
+        if k == 3:
+            for copy in here:
+                copy.wait_recv()
+            return
+        for copy, onward in zip(here, ag_copies(*where, k + 1)):
             copy.wait_recv()
+            onward.start()
 
     def ag_drain(*args):
         for k in range(4):
@@ -336,7 +343,7 @@
         other = 1 - c
         kv_copies.append(kv_copy(6, other, jnp.where(c == 1, x, y) * 2 + c, sibling))
         q_copies.append(q_copy(6, other, jnp.where(c == 1, y, x) * 2 + c, sibling))
-        for i, step in enumerate((1, 3, 2)):
+        for i, step in enumerate((3, 2, 1)):
             kv_copies.append(kv_copy(i, 0, x * 2 + c, sid(ring(x, step), y, 0)))
             kv_copies.append(kv_copy(3 + i, 1, y * 2 + c, sid(x, ring(y, step), 1)))
             q_copies.append(q_copy(i, 0, y * 2 + c, sid(x, ring(y, step), 0)))
@@ -345,33 +352,44 @@
 
     def exchange_start(p):
         rows = group_rows(p)
-        kv_copies, q_copies = exchange(p)
-        for copy in q_copies + kv_copies:
+        for copy in exchange(p)[0]:
             copy.start()
         kv_buf[slot_rows(a0 * 2 + c, p), :] = kv_send[c, rows, :]
         q_buf[slot_rows(b0 * 2 + c, p), :] = q_send[c, rows, :]
 
-    def exchange_wait(p, want_q, want_kv):
+    def queries_start():
+        copies = [exchange(p)[1] for p in range(PARTS)]
+        for i in (1, 2, 3, 4, 5, 6, 0):
+            for p in range(PARTS):
+                copies[p][i].start()
+
+    def queries_wait(b):
+        @pl.loop(0, 2)
+        def _(core):
+            slot = b * 2 + core
+
+            @pl.when(slot != b0 * 2 + c)
+            def _():
+                for p in range(PARTS):
+                    remote(
+                        q_send.at[0, group_rows(p)],
+                        q_buf.at[slot_rows(slot, p)],
+                        q_ssem.at[p, 0],
+                        q_rsem.at[p, slot],
+                        seq=sibling,
+                    ).wait_recv()
+
+    def exchange_wait(p):
         rows = group_rows(p)
         for i in range(1, 8):
-            if want_q:
-                slot = (b0 * 2 + c + i) & 7
-                remote(
-                    q_send.at[0, rows],
-                    q_buf.at[slot_rows(slot, p)],
-                    q_ssem.at[p, 0],
-                    q_rsem.at[p, slot],
-                    seq=sibling,
-                ).wait_recv()
-            if want_kv:
-                slot = (a0 * 2 + c + i) & 7
-                remote(
-                    kv_send.at[0, rows],
-                    kv_buf.at[slot_rows(slot, p)],
-                    kv_ssem.at[p, 0],
-                    kv_rsem.at[p, slot],
-                    seq=sibling,
-                ).wait_recv()
+            slot = (a0 * 2 + c + i) & 7
+            remote(
+                kv_send.at[0, rows],
+                kv_buf.at[slot_rows(slot, p)],
+                kv_ssem.at[p, 0],
+                kv_rsem.at[p, slot],
+                seq=sibling,
+            ).wait_recv()
 
     def exchange_drain(p):
         kv_copies, q_copies = exchange(p)
@@ -498,6 +516,7 @@
         def _():
             @pl.loop(0, first_plain)
             def _(b):
+                queries_wait(b)
                 masked_block(b, jnp.where(jnp.logical_and(c == 0, b < 3), 1, 3))
                 give_block(b)
 
@@ -506,9 +525,14 @@
             turn = b0 + i - first_plain
             turn = jnp.where(turn >= 3, turn - 3, turn)
             b = jnp.where(c == 0, (b0 + 1 + i) & 3, 1 + turn)
+            queries_wait(b)
             plain_slot(b * 2)
             plain_slot(b * 2 + 1)
             give_block(b)
+
+        @pl.when(nothing)
+        def _():
+            queries_wait(0)
 
     def give_wait(p):
         for i in range(1, 8):
@@ -653,16 +677,14 @@
             yield
         mix(p)
         ag_start(*mix_args[p], 0)
+        yield
         up_part(p, z, own=True)
-        yield
         for k in range(4):
-            ag_wait(*mix_args[p], k)
+            ag_step(*mix_args[p], k)
             if k < 3:
-                ag_start(*mix_args[p], k + 1)
+                yield
+                up_part(p, (z + 1 + k) & 7)
             up_part(p, (z - 1 - k) & 7)
-            if k < 3:
-                up_part(p, (z + 1 + k) & 7)
-                yield
         activate(p)
         for k in range(4):
             rs_step(p, 1, down_block(p), k)
@@ -671,29 +693,29 @@
         yield
 
     for k in range(4):
-        ag_wait(*emb_args, k)
-        if k < 3:
-            ag_start(*emb_args, k + 1)
+        ag_step(*emb_args, k)
         for p in range(PARTS):
-            ag_wait(*pos_args[p], k)
-            if k < 3:
-                ag_start(*pos_args[p], k + 1)
-            if k > 0:
-                embed_work(p, k - 1)
+            ag_step(*pos_args[p], k)
             if k == 3:
                 embed_work(p, k)
                 project(p)
                 exchange_start(p)
+        if 0 < k < 3:
+            for p in range(PARTS):
+                embed_work(p, k - 1)
+                if k == 2:
+                    embed_work(p, k)
         if k == 0:
             wait_cells()
             pool_inputs()
             weights[0].wait()
             for p in range(PARTS):
                 embed_block(p, z, own=True)
+    queries_start()
     for i in range(1, 4):
         weights[i].wait()
     for p in range(PARTS):
-        exchange_wait(p, True, True)
+        exchange_wait(p)
     attend()
     chains = [chain(p) for p in range(PARTS)]
     while chains:

time: 113 us -> 110 us (0.973)
  Pallas kernels: 111 us -> 108 us
    pallas_call x1, Pallas kernels: 111 us -> 108 us  [body(): pl.pallas_call(kernel, out_shape=jax.ShapeDtypeStruct((TOK, FB), BF), in_...]
where the time goes in v4:
time: 110 us
  Pallas kernels  108 us (98%)
  local copies, waits for them, and re-layouts  1.6 us (1%)
    pallas_call x1, Pallas kernels, body(): pl.pallas_call(kernel, out_shape=jax.ShapeDtypeStruct((TOK, FB), BF), in_...  108 us

profile of v4, /device:TPU:6, one launch (start us, length us, event | category | flops | bytes accessed | tf_op | source)
XLA Modules:
  0.0 110.0 jit_solution(10860655888673818436)
XLA Ops:
  0.0 108.4 %shard_map.91 = bf16[336,256]{1,0:T(8,128)(2,1)} custom-call(bf16[2,4096]{1,0:T(2,128)(2,1)} %latent_ref.1, bf16[336,256]{1,0:T(8,128)(2,1)} %pos_hbm.1, bf16[32,256]{1,0:T(8,128)(2,1)} %embed_hbm.1, f32[1,2048]{1,0:T(1,128)} %bitcast.2, bf16[3,2048,256]{2,1,0:T(8,128)(2,1)} %qkv_hbm.1, bf16[256,2048]{1,0:T(8,128)(2,1)} %out_w_hbm.1, f32[1,2048]{1,0:T(1,128)} %bitcast.3, ...), custom_call_target="tpu_custom_call" | custom-call | tf_op jit(solution)/shard_map/pallas_call | solution.py:742
  108.4 1.6 %copy.11 = bf16[336,256]{1,0:T(8,128)(2,1)} copy(bf16[336,256]{1,0:T(8,128)(2,1)} %shard_map.91) | data formatting | bytes 344064

commit v5 on v4

--- a/solution.py
+++ b/solution.py
@@ -717,21 +717,22 @@
     for p in range(PARTS):
         exchange_wait(p)
     attend()
+    late = [lambda: (each_taker(lambda copy: copy.wait_send()), ag_drain(*emb_args))]
+    late += [functools.partial(ag_drain, *pos_args[p]) for p in range(PARTS)]
+    late += [functools.partial(exchange_drain, p) for p in range(PARTS)]
+    late += [give_drain]
+    late += [lambda: [rs_drain(p, 0) for p in range(PARTS)]]
+    late += [lambda: None]
+    late += [lambda: [ag_drain(*mix_args[p]) for p in range(PARTS)]]
     chains = [chain(p) for p in range(PARTS)]
     while chains:
         for each in list(chains):
             if next(each, 0) == 0:
                 chains.remove(each)
-
-    each_taker(lambda copy: copy.wait_send())
-    give_drain()
-    ag_drain(*emb_args)
-    for g in range(PARTS):
-        exchange_drain(g)
+        if late:
+            late.pop(0)()
+
     for p in range(PARTS):
-        ag_drain(*pos_args[p])
-        rs_drain(p, 0)
-        ag_drain(*mix_args[p])
         rs_drain(p, 1)
 
 

time: 110 us -> 110 us (level)
  no operation moved by 1% of the time
where the time goes in v5:
time: 110 us
  Pallas kernels  108 us (98%)
  local copies, waits for them, and re-layouts  1.6 us (1%)
    pallas_call x1, Pallas kernels, body(): pl.pallas_call(kernel, out_shape=jax.ShapeDtypeStruct((TOK, FB), BF), in_...  108 us

profile of v5, /device:TPU:6, one launch (start us, length us, event | category | flops | bytes accessed | tf_op | source)
XLA Modules:
  0.0 109.9 jit_solution(11153021426159990664)
XLA Ops:
  0.0 108.3 %shard_map.91 = bf16[336,256]{1,0:T(8,128)(2,1)} custom-call(bf16[2,4096]{1,0:T(2,128)(2,1)} %latent_ref.1, bf16[336,256]{1,0:T(8,128)(2,1)} %pos_hbm.1, bf16[32,256]{1,0:T(8,128)(2,1)} %embed_hbm.1, f32[1,2048]{1,0:T(1,128)} %bitcast.2, bf16[3,2048,256]{2,1,0:T(8,128)(2,1)} %qkv_hbm.1, bf16[256,2048]{1,0:T(8,128)(2,1)} %out_w_hbm.1, f32[1,2048]{1,0:T(1,128)} %bitcast.3, ...), custom_call_target="tpu_custom_call" | custom-call | tf_op jit(solution)/shard_map/pallas_call | solution.py:743
  108.3 1.6 %copy.11 = bf16[336,256]{1,0:T(8,128)(2,1)} copy(bf16[336,256]{1,0:T(8,128)(2,1)} %shard_map.91) | data formatting | bytes 344064
